TPU v7x, 512 devices: a whole 4x4x16 slice. The times are simulated.
512 devices in a mesh: exp: 64 (over x, z), ctx: 8 (over y, core).
Axes of the slice: x: 4, y: 4, z: 16, core: 2. Of those that a mesh axis runs over, the one named last changes fastest.
Arguments:
- y_first: bfloat16 [8192, 1024], P('exp', 'ctx'), may hold values from -6 to 6
- y_second: bfloat16 [8192, 1024], P('exp', 'ctx'), may hold values from -6 to 6
- grad_first: bfloat16 [8192, 1024], P('exp', 'ctx'), may hold values from -6 to 6
- grad_second: bfloat16 [8192, 1024], P('exp', 'ctx'), may hold values from -6 to 6
- expert_ids: int32 [8192, 6], P('exp'), may hold values from 0 to 63, all different within a row; in each aligned block of 128 rows (0 to 127, 128 to 255, ...) at most 16 rows name the same one
- gate_fixed: int32 [8192, 6], P('exp'), may hold values from 4096 to 65535
- gain_attn: float32 [1024], replicated, may hold values from 0.5 to 1.5
- gain_latent: float32 [512], replicated, may hold values from 0.5 to 1.5
- gain_moe: float32 [1024], replicated, may hold values from 0.5 to 1.5
- w_query: bfloat16 [1024, 1024], P(None, 'ctx'), may hold values from -0.1875 to 0.1875
- w_latent: bfloat16 [1024, 512], P(None, 'ctx'), may hold values from -0.1875 to 0.1875
- w_key_up: bfloat16 [512, 1024], P(None, 'ctx'), may hold values from -0.25 to 0.25
- w_value_up: bfloat16 [512, 1024], P(None, 'ctx'), may hold values from -0.25 to 0.25
- w_out: bfloat16 [1024, 1024], P('ctx'), may hold values from -0.1875 to 0.1875
- w_gate: bfloat16 [64, 1024, 1408], P('exp', None, 'ctx'), may hold values from -0.1875 to 0.1875
- w_up: bfloat16 [64, 1024, 1408], P('exp', None, 'ctx'), may hold values from -0.1875 to 0.1875
- w_down: bfloat16 [64, 1408, 1024], P('exp', 'ctx'), may hold values from -0.15625 to 0.15625
Outputs:
- first_out: bfloat16 [8192, 1024], P('exp', 'ctx')
- second_out: bfloat16 [8192, 1024], P('exp', 'ctx')
- grad_first_out: bfloat16 [8192, 1024], P('exp', 'ctx')
- grad_second_out: bfloat16 [8192, 1024], P('exp', 'ctx')
Inputs may be any that keep to these rules, and one draw needn't show every extreme that they name: `expert_ids`: each row names 6 different experts. In each aligned block of 128 rows (one window, the rows of one index of exp) no expert is named by more than 16 rows, a bound that some expert reaches in every block.
All inputs are finite; a program needn't handle non-finite values.
Results may differ from a plain program's by a relative error of at most 0.025.
Values may be sent and summed in bfloat16 or wider, within the bound.
A program may use at most 64 MiB of HBM per device.

v0:
```python
import math

import jax
import jax.numpy as jnp
from jax import lax
from jax.sharding import PartitionSpec as P

HEAD_DIM = 128
TOP = 6


epsilon = 1e-06
soft_limit = 5.0


def rms_scale(row_data):
    return lax.rsqrt(jnp.mean(row_data * row_data, axis=-1, keepdims=True) + epsilon)


def rms_back(row_data, gain_vec, grad_in):
    factor = rms_scale(row_data)
    weighted = gain_vec * grad_in
    inner_mean = jnp.mean(weighted * row_data, axis=-1, keepdims=True)
    return factor * weighted - row_data * (factor * factor * factor) * inner_mean


def route_slots(expert_rows, expert_count):
    flat_ids = expert_rows.reshape(-1)
    labels = jnp.arange(expert_count)
    onehot = (flat_ids[:, None] == labels[None, :]).astype(jnp.int32)
    before = jnp.cumsum(onehot, axis=0) - onehot
    return jnp.sum(before * onehot, axis=1).reshape(expert_rows.shape)


def local(
    y_first,
    y_second,
    grad_first,
    grad_second,
    expert_ids,
    gate_fixed,
    gain_attn,
    gain_latent,
    gain_moe,
    w_query,
    w_latent,
    w_key_up,
    w_value_up,
    w_out,
    w_gate,
    w_up,
    w_down,
):
    ctx_count = lax.axis_size("ctx")
    exp_count = lax.axis_size("exp")
    ctx_index = lax.axis_index("ctx")
    local_experts = w_gate.shape[0]
    expert_count = exp_count * local_experts
    window_len = y_first.shape[0]
    own_cols = y_first.shape[1]
    model_width = own_cols * ctx_count
    capacity = ctx_count * (
        (window_len * TOP * 4 + 3 * expert_count * ctx_count - 1) // (3 * expert_count * ctx_count)
    )
    full_first, full_second, full_gfirst, full_gsecond = (
        lax.all_gather(y_first, "ctx", axis=1, tiled=True),
        lax.all_gather(y_second, "ctx", axis=1, tiled=True),
        lax.all_gather(grad_first, "ctx", axis=1, tiled=True),
        lax.all_gather(grad_second, "ctx", axis=1, tiled=True),
    )
    first_in = full_first.astype(jnp.float32)
    normed = (first_in * rms_scale(first_in) * gain_moe).astype(jnp.bfloat16)
    slot_ids = route_slots(expert_ids, expert_count)
    flat_slots = (expert_ids * capacity + slot_ids).reshape(-1)
    targets = jnp.arange(expert_count * capacity)
    hits = (targets[:, None] == flat_slots[None, :]).astype(jnp.bfloat16)
    chooser = jnp.max(hits.reshape(expert_count * capacity, window_len, TOP), axis=2)
    send_rows = jnp.dot(chooser, normed, preferred_element_type=jnp.float32).astype(jnp.bfloat16)
    send_rows = send_rows.reshape(expert_count, capacity, model_width)
    send_grads = jnp.dot(chooser, full_gsecond, preferred_element_type=jnp.float32).astype(
        jnp.bfloat16
    )
    send_grads = send_grads.reshape(expert_count, capacity, model_width)
    recv_rows, recv_grads = (
        lax.all_to_all(send_rows, "exp", split_axis=0, concat_axis=0, tiled=True),
        lax.all_to_all(send_grads, "exp", split_axis=0, concat_axis=0, tiled=True),
    )
    grouped_rows = recv_rows.reshape(exp_count, local_experts, capacity, model_width)
    grouped_grads = recv_grads.reshape(exp_count, local_experts, capacity, model_width)
    gate_proj = jnp.einsum(
        "secd,edf->secf", grouped_rows, w_gate, preferred_element_type=jnp.float32
    )
    up_proj = jnp.einsum("secd,edf->secf", grouped_rows, w_up, preferred_element_type=jnp.float32)
    sigmoid_gate = jax.nn.sigmoid(gate_proj)
    hidden = (gate_proj * sigmoid_gate * up_proj).astype(jnp.bfloat16)
    part_out = jnp.einsum(
        "secf,efd->secd", hidden, w_down, preferred_element_type=jnp.float32
    ).astype(jnp.bfloat16)
    grad_hidden = jnp.einsum(
        "secd,efd->secf", grouped_grads, w_down, preferred_element_type=jnp.float32
    )
    grad_gate = (
        grad_hidden * up_proj * sigmoid_gate * (1.0 + gate_proj * (1.0 - sigmoid_gate))
    ).astype(jnp.bfloat16)
    grad_up = (grad_hidden * gate_proj * sigmoid_gate).astype(jnp.bfloat16)
    part_back = jnp.einsum("secf,edf->secd", grad_gate, w_gate, preferred_element_type=jnp.float32)
    part_back = part_back + jnp.einsum(
        "secf,edf->secd", grad_up, w_up, preferred_element_type=jnp.float32
    )
    part_back = part_back.astype(jnp.bfloat16)
    weights = gate_fixed.astype(jnp.float32) / 65536.0
    back_out, back_grads = (
        lax.all_to_all(
            part_out.reshape(expert_count, capacity, model_width),
            "exp",
            split_axis=0,
            concat_axis=0,
            tiled=True,
        ),
        lax.all_to_all(
            part_back.reshape(expert_count, capacity, model_width),
            "exp",
            split_axis=0,
            concat_axis=0,
            tiled=True,
        ),
    )
    picked_out = jnp.take(
        back_out.reshape(expert_count * capacity, model_width), flat_slots, axis=0
    )
    picked_out = picked_out.reshape(window_len, TOP, model_width).astype(jnp.float32)
    picked_grads = jnp.take(
        back_grads.reshape(expert_count * capacity, model_width), flat_slots, axis=0
    )
    picked_grads = picked_grads.reshape(window_len, TOP, model_width).astype(jnp.float32)
    moe_part = jnp.sum(weights[:, :, None] * picked_out, axis=1)
    grad_part = jnp.sum(weights[:, :, None] * picked_grads, axis=1)
    moe_out, grad_moe = (
        lax.psum(moe_part.astype(jnp.bfloat16), "ctx").astype(jnp.float32),
        lax.psum(grad_part.astype(jnp.bfloat16), "ctx").astype(jnp.float32),
    )
    second_full = (full_second.astype(jnp.float32) - moe_out).astype(jnp.bfloat16)
    total_grad = full_gfirst.astype(jnp.float32) + rms_back(first_in, gain_moe, grad_moe)
    grad_first_full = total_grad.astype(jnp.bfloat16)
    second = second_full.astype(jnp.float32)
    attn_in = (second * rms_scale(second) * gain_attn).astype(jnp.bfloat16)
    queries = jnp.dot(attn_in, w_query, preferred_element_type=jnp.float32).astype(jnp.bfloat16)
    latent_part = jnp.dot(attn_in, w_latent, preferred_element_type=jnp.float32).astype(
        jnp.bfloat16
    )
    latent = lax.all_gather(latent_part, "ctx", axis=1, tiled=True)
    latent_f = latent.astype(jnp.float32)
    latent_norm = (latent_f * rms_scale(latent_f) * gain_latent).astype(jnp.bfloat16)
    key_rows = jnp.dot(latent_norm, w_key_up, preferred_element_type=jnp.float32).astype(
        jnp.bfloat16
    )
    value_rows = jnp.dot(latent_norm, w_value_up, preferred_element_type=jnp.float32).astype(
        jnp.bfloat16
    )
    local_heads = w_query.shape[1] // HEAD_DIM
    head_shape = (window_len, local_heads, HEAD_DIM)
    query_heads = queries.reshape(head_shape)
    key_heads = key_rows.reshape(head_shape)
    value_heads = value_rows.reshape(head_shape)
    scale_factor = 1.0 / math.sqrt(HEAD_DIM)
    raw_scores = (
        jnp.einsum("qhk,shk->hqs", query_heads, key_heads, preferred_element_type=jnp.float32)
        * scale_factor
    )
    bounded = jnp.tanh(raw_scores / soft_limit)
    positions = jnp.arange(window_len)
    allowed = positions[None, :] <= positions[:, None]
    exp_scores = jnp.where(allowed[None], jnp.exp(soft_limit * bounded), 0.0)
    probs_full = exp_scores / jnp.sum(exp_scores, axis=-1, keepdims=True)
    probs_low = probs_full.astype(jnp.bfloat16)
    mixed_heads = jnp.einsum(
        "hqs,shk->qhk", probs_low, value_heads, preferred_element_type=jnp.float32
    )
    mixed_heads = mixed_heads.astype(jnp.bfloat16).reshape(window_len, local_heads * HEAD_DIM)
    attn_part = jnp.dot(mixed_heads, w_out, preferred_element_type=jnp.float32)
    attn_out = lax.psum_scatter(
        attn_part.astype(jnp.bfloat16), "ctx", scatter_dimension=1, tiled=True
    ).astype(jnp.float32)
    first_out = (y_first.astype(jnp.float32) - attn_out).astype(jnp.bfloat16)
    grad_mixed = jnp.einsum(
        "td,hd->th", grad_first_full, w_out, preferred_element_type=jnp.float32
    ).astype(jnp.bfloat16)
    grad_heads = grad_mixed.reshape(head_shape)
    grad_probs = jnp.einsum(
        "qhk,shk->hqs", grad_heads, value_heads, preferred_element_type=jnp.float32
    )
    row_delta = jnp.sum(probs_full * grad_probs, axis=-1, keepdims=True)
    grad_scores = (
        probs_full * (grad_probs - row_delta) * (1.0 - bounded * bounded) * scale_factor
    ).astype(jnp.bfloat16)
    flat_width = local_heads * HEAD_DIM
    grad_queries = jnp.einsum(
        "hqs,shk->qhk", grad_scores, key_heads, preferred_element_type=jnp.float32
    )
    grad_queries = grad_queries.astype(jnp.bfloat16).reshape(window_len, flat_width)
    grad_keys = jnp.einsum(
        "hqs,qhk->shk", grad_scores, query_heads, preferred_element_type=jnp.float32
    )
    grad_keys = grad_keys.astype(jnp.bfloat16).reshape(window_len, flat_width)
    grad_values = jnp.einsum(
        "hqs,qhk->shk", probs_low, grad_heads, preferred_element_type=jnp.float32
    )
    grad_values = grad_values.astype(jnp.bfloat16).reshape(window_len, flat_width)
    latent_grad_part = jnp.einsum(
        "th,lh->tl", grad_keys, w_key_up, preferred_element_type=jnp.float32
    )
    latent_grad_part = latent_grad_part + jnp.einsum(
        "th,lh->tl", grad_values, w_value_up, preferred_element_type=jnp.float32
    )
    grad_latent_norm = lax.psum(latent_grad_part.astype(jnp.bfloat16), "ctx").astype(jnp.float32)
    grad_latent = rms_back(latent_f, gain_latent, grad_latent_norm).astype(jnp.bfloat16)
    latent_cols = w_latent.shape[1]
    own_latent = lax.dynamic_slice_in_dim(grad_latent, ctx_index * latent_cols, latent_cols, 1)
    input_part = jnp.einsum("th,dh->td", grad_queries, w_query, preferred_element_type=jnp.float32)
    input_part = input_part + jnp.einsum(
        "tl,dl->td", own_latent, w_latent, preferred_element_type=jnp.float32
    )
    grad_attn_in = lax.psum(input_part.astype(jnp.bfloat16), "ctx").astype(jnp.float32)
    full_back = rms_back(second, gain_attn, grad_attn_in)
    own_back = lax.dynamic_slice_in_dim(full_back, ctx_index * own_cols, own_cols, 1)
    grad_second_out = (grad_second.astype(jnp.float32) + own_back).astype(jnp.bfloat16)
    second_out = lax.dynamic_slice_in_dim(second_full, ctx_index * own_cols, own_cols, 1)
    grad_first_out = lax.dynamic_slice_in_dim(grad_first_full, ctx_index * own_cols, own_cols, 1)
    return (first_out, second_out, grad_first_out, grad_second_out)


def solution(mesh):
    placed = (
        P("exp", "ctx"),
        P("exp", "ctx"),
        P("exp", "ctx"),
        P("exp", "ctx"),
        P("exp", None),
        P("exp", None),
        P(),
        P(),
        P(),
        P(None, "ctx"),
        P(None, "ctx"),
        P(None, "ctx"),
        P(None, "ctx"),
        P("ctx", None),
        P("exp", None, "ctx"),
        P("exp", None, "ctx"),
        P("exp", "ctx", None),
    )
    return jax.shard_map(
        local,
        mesh=mesh,
        in_specs=placed,
        out_specs=(P("exp", "ctx"), P("exp", "ctx"), P("exp", "ctx"), P("exp", "ctx")),
        check_vma=False,
    )
```

profile of v0, /device:TPU:1, one launch (start us, length us, event | category | flops | bytes accessed | tf_op | source)
XLA Modules:
  0.0 781.6 jit_solution(9239729217433142094)
XLA Ops:
  8.3 1.8 reduce-window.6
  11.8 18.4 %all_gather.16 = bf16[128,1024]{1,0:T(8,128)(2,1)S(1)} all-gather(bf16[128,128]{1,0:T(8,128)(2,1)} %param.19), channel_id=1, replica_groups=mesh['exp'=64,'ctx'=8] {'ctx'}, dimensions={1}, use_global_device_ids=true | all-gather | bytes 294912 | tf_op jit(solution)/shard_map/all_gather | solution.py:66
  31.0 2.1 convolution_convert_fusion.2
  33.1 13.9 %all-to-all-start = ((bf16[64,16,1024]{2,1,0:T(8,128)(2,1)}), bf16[64,16,1024]{2,1,0:T(8,128)(2,1)S(1)}, u32[]{:S(2)}, u32[]{:S(2)}) async-start(bf16[64,16,1024]{2,1,0:T(8,128)(2,1)} %bitcast.132), calls=%async_computation | async-start | bytes 4194304 | tf_op jit(solution)/shard_map/all_to_all | solution.py:85
  47.1 11.8 %all_gather.19 = bf16[128,1024]{1,0:T(8,128)(2,1)S(1)} all-gather(bf16[128,128]{1,0:T(8,128)(2,1)S(1)} %copy-done.11), channel_id=1, replica_groups=mesh['exp'=64,'ctx'=8] {'ctx'}, dimensions={1}, use_global_device_ids=true | all-gather | bytes 294912 | tf_op jit(solution)/shard_map/all_gather | solution.py:69
  58.9 2.0 convolution_convert_fusion.1
  60.9 78.2 %all-to-all-done = bf16[64,16,1024]{2,1,0:T(8,128)(2,1)S(1)} async-done(((bf16[64,16,1024]{2,1,0:T(8,128)(2,1)}), bf16[64,16,1024]{2,1,0:T(8,128)(2,1)S(1)}, u32[]{:S(2)}, u32[]{:S(2)}) %all-to-all-start) | async-done | bytes 2097184 | tf_op jit(solution)/shard_map/all_to_all | solution.py:85
  139.1 13.9 %all-to-all-start.2 = ((bf16[64,16,1024]{2,1,0:T(8,128)(2,1)}), bf16[64,16,1024]{2,1,0:T(8,128)(2,1)}, u32[]{:S(2)}, u32[]{:S(2)}) async-start(bf16[64,16,1024]{2,1,0:T(8,128)(2,1)} %bitcast.131), calls=%async_computation.2 | async-start | bytes 4194304 | tf_op jit(solution)/shard_map/all_to_all | solution.py:86
  154.0 1.7 convolution_bitcast_fusion.1
  155.7 92.4 %all-to-all-done.2 = bf16[64,16,1024]{2,1,0:T(8,128)(2,1)} async-done(((bf16[64,16,1024]{2,1,0:T(8,128)(2,1)}), bf16[64,16,1024]{2,1,0:T(8,128)(2,1)}, u32[]{:S(2)}, u32[]{:S(2)}) %all-to-all-start.2) | async-done | bytes 2097184 | tf_op jit(solution)/shard_map/all_to_all | solution.py:86
  248.1 2.3 convolution_bitcast_fusion
  251.5 2.1 add_convert_fusion
  253.6 10.4 %all-to-all-start.3 = ((bf16[64,16,1024]{2,1,0:T(8,128)(2,1)}), bf16[64,16,1024]{2,1,0:T(8,128)(2,1)S(1)}, u32[]{:S(2)}, u32[]{:S(2)}) async-start(bf16[64,16,1024]{2,1,0:T(8,128)(2,1)} %add_convert_fusion), calls=%async_computation.3 | async-start | bytes 4194304 | tf_op jit(solution)/shard_map/all_to_all | solution.py:120
  264.0 3.4 convolution_convert_fusion
  267.4 91.7 %all-to-all-done.3 = bf16[64,16,1024]{2,1,0:T(8,128)(2,1)S(1)} async-done(((bf16[64,16,1024]{2,1,0:T(8,128)(2,1)}), bf16[64,16,1024]{2,1,0:T(8,128)(2,1)S(1)}, u32[]{:S(2)}, u32[]{:S(2)}) %all-to-all-start.3) | async-done | bytes 2097184 | tf_op jit(solution)/shard_map/all_to_all | solution.py:120
  359.2 10.8 %all-to-all-start.1 = ((bf16[64,16,1024]{2,1,0:T(8,128)(2,1)}), bf16[64,16,1024]{2,1,0:T(8,128)(2,1)}, u32[]{:S(2)}, u32[]{:S(2)}) async-start(bf16[64,16,1024]{2,1,0:T(8,128)(2,1)} %convolution_convert_fusion), calls=%async_computation.1 | async-start | bytes 4194304 | tf_op jit(solution)/shard_map/all_to_all | solution.py:113
  371.3 3.6 gather_fusion.1
  374.9 90.0 %all-to-all-done.1 = bf16[64,16,1024]{2,1,0:T(8,128)(2,1)} async-done(((bf16[64,16,1024]{2,1,0:T(8,128)(2,1)}), bf16[64,16,1024]{2,1,0:T(8,128)(2,1)}, u32[]{:S(2)}, u32[]{:S(2)}) %all-to-all-start.1) | async-done | bytes 2097184 | tf_op jit(solution)/shard_map/all_to_all | solution.py:113
  464.9 6.4 gather_fusion
  471.3 4.0 select_convert_fusion.1
  475.4 4.6 reshape.255
  480.0 2.2 reshape.256
  482.1 7.5 multiply_reduce_fusion
  489.8 14.9 %all_gather.18 = bf16[128,1024]{1,0:T(8,128)(2,1)S(1)} all-gather(bf16[128,128]{1,0:T(8,128)(2,1)S(1)} %copy-done.15), channel_id=1, replica_groups=mesh['exp'=64,'ctx'=8] {'ctx'}, dimensions={1}, use_global_device_ids=true | all-gather | bytes 294912 | tf_op jit(solution)/shard_map/all_gather | solution.py:68
  504.7 11.9 %all_gather.15 = bf16[128,1024]{1,0:T(8,128)(2,1)S(1)} all-gather(bf16[128,128]{1,0:T(8,128)(2,1)S(1)} %copy-done.16), channel_id=1, replica_groups=mesh['exp'=64,'ctx'=8] {'ctx'}, dimensions={1}, use_global_device_ids=true | all-gather | bytes 294912 | tf_op jit(solution)/shard_map/all_gather | solution.py:67
  516.6 43.6 %all-reduce.9.cloned.1.call-done = (bf16[128,1024]{1,0:T(8,128)(2,1)}, bf16[128,1024]{1,0:T(8,128)(2,1)}) async-done(((bf16[128,1024]{1,0:T(8,128)(2,1)}, bf16[128,1024]{1,0:T(8,128)(2,1)}), (bf16[128,1024]{1,0:T(8,128)(2,1)}, bf16[128,1024]{1,0:T(8,128)(2,1)})) %all-reduce.9.cloned.1.call-update) | async-done | bytes 524304 | tf_op jit(solution)/shard_map/psum | solution.py:139
  563.4 14.8 %all_gather.17 = bf16[128,512]{0,1:T(8,128)(2,1)S(1)} all-gather(bf16[128,64]{0,1:T(8,128)(2,1)S(1)} %convolution_convert_fusion.12), channel_id=1, replica_groups=mesh['exp'=64,'ctx'=8] {'ctx'}, dimensions={1}, use_global_device_ids=true | all-gather | bytes 147456 | tf_op jit(solution)/shard_map/all_gather | solution.py:151
  581.1 1.2 fusion.7
  583.9 72.3 %all-reduce.5.cloned.1.call-done = bf16[128,512]{0,1:T(8,128)(2,1)} async-done(((bf16[128,512]{0,1:T(8,128)(2,1)}), bf16[128,512]{0,1:T(8,128)(2,1)}) %all-reduce.5.cloned.1.call-update) | async-done | bytes 131088 | tf_op jit(solution)/shard_map/psum | solution.py:215
  657.3 1.6 fusion.2
  661.1 72.4 %all-reduce.7.cloned.1.call-done = bf16[128,1024]{1,0:T(8,128)(2,1)} async-done(((bf16[128,1024]{1,0:T(8,128)(2,1)}), bf16[128,1024]{1,0:T(8,128)(2,1)}) %all-reduce.7.cloned.1.call-update) | async-done | bytes 262160 | tf_op jit(solution)/shard_map/psum | solution.py:223
  735.3 38.2 %reduce-scatter.4.cloned.1.call-done = bf16[128,128]{1,0:T(8,128)(2,1)} async-done(((bf16[1024,128]{1,0:T(8,128)(2,1)}), bf16[128,128]{1,0:T(8,128)(2,1)}) %reduce-scatter.4.cloned.1.call-update) | async-done | bytes 32784
  (114 shorter events, 21.0 us)
Async XLA Ops:
  7.2 145.8 %copy-start = (bf16[1,1024,176]{1,2,0:T(8,128)(2,1)S(1)}, bf16[1,1024,176]{1,2,0:T(8,128)(2,1)}, u32[]{:S(2)}) copy-start(bf16[1,1024,176]{1,2,0:T(8,128)(2,1)} %param.33) | copy-start | bytes 1081348
  7.2 23.8 %copy-start.14 = (f32[1024]{0:T(1024)S(1)}, f32[1024]{0:T(1024)}, u32[]{:S(2)}) copy-start(f32[1024]{0:T(1024)} %param.27) | copy-start | bytes 12292
  33.1 13.9 %copy-start.11 = (bf16[128,128]{1,0:T(8,128)(2,1)S(1)}, bf16[128,128]{1,0:T(8,128)(2,1)}, u32[]{:S(2)}) copy-start(bf16[128,128]{1,0:T(8,128)(2,1)} %param.22) | copy-start | bytes 98308
  33.1 106.0 %all-to-all-start = ((bf16[64,16,1024]{2,1,0:T(8,128)(2,1)}), bf16[64,16,1024]{2,1,0:T(8,128)(2,1)S(1)}, u32[]{:S(2)}, u32[]{:S(2)}) async-start(bf16[64,16,1024]{2,1,0:T(8,128)(2,1)} %bitcast.132), calls=%async_computation | async-start | bytes 4194304 | tf_op jit(solution)/shard_map/all_to_all | solution.py:85
  139.1 109.0 %all-to-all-start.2 = ((bf16[64,16,1024]{2,1,0:T(8,128)(2,1)}), bf16[64,16,1024]{2,1,0:T(8,128)(2,1)}, u32[]{:S(2)}, u32[]{:S(2)}) async-start(bf16[64,16,1024]{2,1,0:T(8,128)(2,1)} %bitcast.131), calls=%async_computation.2 | async-start | bytes 4194304 | tf_op jit(solution)/shard_map/all_to_all | solution.py:86
  155.7 94.7 %copy-start.3 = (f32[64,1,16,176]{3,2,0,1:T(8,128)S(1)}, f32[64,1,16,176]{3,2,0,1:T(8,128)}, u32[]{:S(2)}) copy-start(f32[64,1,16,176]{3,2,0,1:T(8,128)} %convolution_bitcast_fusion.1) | copy-start | bytes 2162692
  253.6 105.5 %all-to-all-start.3 = ((bf16[64,16,1024]{2,1,0:T(8,128)(2,1)}), bf16[64,16,1024]{2,1,0:T(8,128)(2,1)S(1)}, u32[]{:S(2)}, u32[]{:S(2)}) async-start(bf16[64,16,1024]{2,1,0:T(8,128)(2,1)} %add_convert_fusion), calls=%async_computation.3 | async-start | bytes 4194304 | tf_op jit(solution)/shard_map/all_to_all | solution.py:120
  267.4 103.0 %copy-start.19 = (s32[128,6]{0,1:T(8,128)S(1)}, s32[128,6]{0,1:T(8,128)}, u32[]{:S(2)}) copy-start(s32[128,6]{0,1:T(8,128)} %param.24) | copy-start | bytes 9220
  359.2 105.8 %all-to-all-start.1 = ((bf16[64,16,1024]{2,1,0:T(8,128)(2,1)}), bf16[64,16,1024]{2,1,0:T(8,128)(2,1)}, u32[]{:S(2)}, u32[]{:S(2)}) async-start(bf16[64,16,1024]{2,1,0:T(8,128)(2,1)} %convolution_convert_fusion), calls=%async_computation.1 | async-start | bytes 4194304 | tf_op jit(solution)/shard_map/all_to_all | solution.py:113
  370.0 190.2 %all-reduce.9.cloned.1.call-start = ((), (), s32[]{:S(2)}) async-start(), calls=%async_computation.8 | async-start | bytes 1048576 | tf_op jit(solution)/shard_map/psum | solution.py:139
  482.1 7.6 copy-start.15
  482.1 22.5 %copy-start.16 = (bf16[128,128]{1,0:T(8,128)(2,1)S(1)}, bf16[128,128]{1,0:T(8,128)(2,1)}, u32[]{:S(2)}) copy-start(bf16[128,128]{1,0:T(8,128)(2,1)} %param.20) | copy-start | bytes 98308
  482.1 78.1 %copy-start.2 = (bf16[128,1024]{1,0:T(8,128)(2,1)S(1)}, bf16[128,1024]{1,0:T(8,128)(2,1)}, u32[]{:S(2)}) copy-start(bf16[128,1024]{1,0:T(8,128)(2,1)} %copy-done.1) | copy-start | bytes 786436
  489.7 73.4 %copy-start.10 = (bf16[1024,64]{0,1:T(8,128)(2,1)S(1)}, bf16[1024,64]{0,1:T(8,128)(2,1)}, u32[]{:S(2)}) copy-start(bf16[1024,64]{0,1:T(8,128)(2,1)} %param.29) | copy-start | bytes 393220
  489.7 73.4 %copy-start.18 = (f32[1024]{0:T(1024)S(1)}, f32[1024]{0:T(1024)}, u32[]{:S(2)}) copy-start(f32[1024]{0:T(1024)} %param.25) | copy-start | bytes 12292
  489.7 89.1 %copy-start.8 = (bf16[1024,128]{1,0:T(8,128)(2,1)S(1)}, bf16[1024,128]{1,0:T(8,128)(2,1)}, u32[]{:S(2)}) copy-start(bf16[1024,128]{1,0:T(8,128)(2,1)} %param.28) | copy-start | bytes 786436
  489.7 166.5 %all-reduce.5.cloned.1.call-start = ((), (), s32[]{:S(2)}) async-start(), calls=%async_computation.5 | async-start | bytes 262144 | tf_op jit(solution)/shard_map/psum | solution.py:215
  489.8 89.3 %copy-start.9 = (bf16[512,128]{1,0:T(8,128)(2,1)S(1)}, bf16[512,128]{1,0:T(8,128)(2,1)}, u32[]{:S(2)}) copy-start(bf16[512,128]{1,0:T(8,128)(2,1)} %param.30) | copy-start | bytes 393220
  489.8 89.3 %copy-start.20 = (f32[512]{0:T(512)S(1)}, f32[512]{0:T(512)}, u32[]{:S(2)}) copy-start(f32[512]{0:T(512)} %param.26) | copy-start | bytes 6148
  504.7 74.8 %copy-start.13 = (bf16[512,128]{1,0:T(8,128)(2,1)S(1)}, bf16[512,128]{1,0:T(8,128)(2,1)}, u32[]{:S(2)}) copy-start(bf16[512,128]{1,0:T(8,128)(2,1)} %param.31) | copy-start | bytes 393220
  560.2 19.7 %copy-start.6 = (bf16[128,1024]{1,0:T(8,128)(2,1)S(1)}, bf16[128,1024]{1,0:T(8,128)(2,1)}, u32[]{:S(2)}) copy-start(bf16[128,1024]{1,0:T(8,128)(2,1)} %get-tuple-element.8) | copy-start | bytes 786436
  560.2 19.7 %copy-start.21 = (f32[128]{0:T(128)S(1)}, f32[128]{0:T(128)}, u32[]{:S(2)}) copy-start(f32[128]{0:T(128)} %get-tuple-element.21) | copy-start | bytes 1540
  562.4 17.7 %copy-start.7 = (bf16[128,1024]{1,0:T(8,128)(2,1)S(1)}, bf16[128,1024]{1,0:T(8,128)(2,1)}, u32[]{:S(2)}) copy-start(bf16[128,1024]{1,0:T(8,128)(2,1)} %param.32) | copy-start | bytes 786436
  563.1 16.7 %copy-start.23 = (f32[128]{0:T(128)}, f32[128]{0:T(128)S(1)}, u32[]{:S(2)}) copy-start(f32[128]{0:T(128)S(1)} %get-tuple-element.18) | copy-start | bytes 1540
  578.8 1.1 copy-start.26
  579.5 1.3 copy-start.17
  580.6 76.7 %copy-start.25 = (f32[128]{0:T(128)S(1)}, f32[128]{0:T(128)}, u32[]{:S(2)}) copy-start(f32[128]{0:T(128)} %get-tuple-element.19) | copy-start | bytes 1540
  583.4 150.1 %all-reduce.7.cloned.1.call-start = ((), (), s32[]{:S(2)}) async-start(), calls=%async_computation.6 | async-start | bytes 524288 | tf_op jit(solution)/shard_map/psum | solution.py:223
  583.9 150.7 %copy-start.22 = (f32[128]{0:T(128)S(1)}, f32[128]{0:T(128)}, u32[]{:S(2)}) copy-start(f32[128]{0:T(128)} %get-tuple-element.17) | copy-start | bytes 1540
  583.9 150.7 %copy-start.24 = (f32[128]{0:T(128)S(1)}, f32[128]{0:T(128)}, u32[]{:S(2)}) copy-start(f32[128]{0:T(128)} %copy-done.23) | copy-start | bytes 1540
  583.9 190.5 %copy-start.12 = (bf16[128,128]{1,0:T(8,128)(2,1)S(1)}, bf16[128,128]{1,0:T(8,128)(2,1)}, u32[]{:S(2)}) copy-start(bf16[128,128]{1,0:T(8,128)(2,1)} %param.19) | copy-start | bytes 98308
  658.9 114.7 %reduce-scatter.4.cloned.1.call-start = ((), (), s32[]{:S(2)}) async-start(), calls=%async_computation.7 | async-start | bytes 294912
  (3 other events, 2.8 us)
Sparse Core Ops, SparseCore 0:
  489.8 70.3 all-reduce.8
  583.5 72.6 all-reduce.4
  659.0 74.3 all-reduce.6
  736.3 37.2 reduce-scatter.3
where the time goes:
time: 783 us; the launch traced here: 782 us
  waiting for transfers between devices  579 us (74%)
  blocking collectives  71.8 us (9%)
  starting transfers between devices  49.4 us (6%)
  local copies, waits for them, and re-layouts  22.7 us (3%)
  other arithmetic  22.6 us (3%)
  matrix products  21.9 us (3%)
  between operations  14.2 us (2%)
    all_to_all x1, waiting for transfers between devices, local(): lax.all_to_all(send_grads, 'exp', split_axis=0, concat_axis=0, tiled=True)  92.4 us
    all_to_all x1, waiting for transfers between devices, local(): lax.all_to_all(part_back.reshape(expert_count, capacity, model_width), 'e...  91.7 us
    all_to_all x1, waiting for transfers between devices, local(): lax.all_to_all(part_out.reshape(expert_count, capacity, model_width), 'ex...  90 us
    all_to_all x1, waiting for transfers between devices, local(): lax.all_to_all(send_rows, 'exp', split_axis=0, concat_axis=0, tiled=True)  78.2 us
    psum x1, waiting for transfers between devices, local(): lax.psum(input_part.astype(jnp.bfloat16), 'ctx').astype(jnp.float32)  72.4 us
    psum x1, waiting for transfers between devices, local(): lax.psum(latent_grad_part.astype(jnp.bfloat16), 'ctx').astype(jnp.float32)  72.3 us
    psum x1, waiting for transfers between devices, local(): lax.psum(moe_part.astype(jnp.bfloat16), 'ctx').astype(jnp.float32)  43.6 us
    unnamed x5, waiting for transfers between devices  38.3 us
  transfers between devices with their start and end apart: 8, of which 8 were waited for; matrix products, arithmetic and copies ran while one was open for 2% of the time, Pallas kernels for 0%

commit v1 on v0

v1 whole, which is shorter than its diff:
```python
import functools
import math

import jax
import jax.numpy as jnp
from jax import lax
from jax.experimental import pallas as pl
from jax.experimental.pallas import tpu as pltpu
from jax.sharding import PartitionSpec as P

CAP = 16
N_CTX = 8
EPS = 1e-06
LIMIT = 5.0
MESH = pl.DeviceIdType.MESH
F32 = jnp.float32
BF16 = jnp.bfloat16


def dot_nn(a, b):
    return lax.dot_general(a, b, (((1,), (0,)), ((), ())), preferred_element_type=F32)


def dot_nt(a, b):
    return lax.dot_general(a, b, (((1,), (1,)), ((), ())), preferred_element_type=F32)


def dot_tn(a, b):
    return lax.dot_general(a, b, (((0,), (0,)), ((), ())), preferred_element_type=F32)


def scale_of(v):
    return lax.rsqrt(jnp.mean(v * v, axis=-1, keepdims=True) + EPS)


def iota(shape, axis):
    return lax.broadcasted_iota(jnp.int32, shape, axis)


def wide(ref, count):
    return jnp.concatenate([ref[i] for i in range(count)], axis=1)


def kernel(
    n_x,
    n_z,
    cap,
    yf_ref,
    ys_ref,
    gf_ref,
    gs_ref,
    ids_ref,
    gate_ref,
    g_attn,
    g_lat,
    g_moe,
    wq,
    wl,
    wk,
    wv,
    wo,
    wg,
    wu,
    wd,
    first_out,
    second_out,
    gfirst_out,
    gsecond_out,
    yf_all,
    gf_all,
    gs_grp,
    ys_grp,
    wg_all,
    wu_all,
    wd_all,
    comb,
    rows_send,
    grads_send,
    rows_in,
    grads_in,
    up_keep,
    gate_keep,
    xo_send,
    xo_recv,
    out_ret,
    out_back,
    xb_send,
    xb_recv,
    bk_ret,
    bk_back,
    sec,
    gm,
    lat_all,
    ao_send,
    ao_recv,
    gff,
    lg_send,
    lg_recv,
    ia_send,
    ia_recv,
    yf_s,
    yf_r,
    gf_s,
    gf_r,
    grp_s,
    grp_r,
    w_s,
    w_r,
    disp_s,
    disp_r,
    cross_s,
    cross_r,
    ret_s,
    ret_r,
    sec_s,
    sec_r,
    gm_s,
    gm_r,
    lat_s,
    lat_r,
    ao_s,
    ao_r,
    lg_s,
    lg_r,
    ia_s,
    ia_r,
):
    n_exp = n_x * n_z
    zi_n = n_z // 4
    wins = n_x * zi_n
    me = lax.axis_index("exp")
    c = lax.axis_index("ctx")
    mx, mz = me // n_z, me % n_z
    y, k = c // 2, c % 2
    p, j = c // 4, c % 4
    q = 2 * (((y + 1) // 2) % 2) + k
    mate = c + 1 - 2 * k
    nbr = c + 2 - 4 * (y % 2)
    cross = 6 - 2 * y + k
    quarter = (mx + mz) % 4
    my_wi = mx * zi_n + mz // 4
    active = q == quarter
    qm, qk = quarter // 2, quarter % 2
    act = 2 * (p * (3 - 2 * qm) + qm) + qk
    half = pl.ds(pl.multiple_of(p * 512, 512), 512)
    other = pl.ds(pl.multiple_of((1 - p) * 512, 512), 512)

    def remote(src, dst, ssem, rsem, e, cc):
        return pltpu.make_async_remote_copy(
            src_ref=src,
            dst_ref=dst,
            send_sem=ssem,
            recv_sem=rsem,
            device_id=(e, cc),
            device_id_type=MESH,
        )

    def wait_bytes(ref, sem):
        pltpu.make_async_copy(ref, ref, sem).wait()

    def shifted(i):
        a, dx = i // n_x, i % n_x
        dz = (a % 2) * ((a + 1) // 2) + (1 - a % 2) * (n_z - a // 2)
        return ((mx + dx) % n_x) * n_z + (mz + dz) % n_z

    barrier = pltpu.get_barrier_semaphore()

    @pl.loop(1, n_exp)
    def _(i):
        pl.semaphore_signal(barrier, inc=1, device_id=(shifted(i), c), device_id_type=MESH)

    @pl.loop(1, N_CTX)
    def _(d):
        pl.semaphore_signal(barrier, inc=1, device_id=(me, (c + d) % N_CTX), device_id_type=MESH)

    yf_all[c] = yf_ref[...]
    gf_all[c] = gf_ref[...]
    gs_grp[j] = gs_ref[...]
    ys_grp[j] = ys_ref[...]
    wg_all[j] = wg[0]
    wu_all[j] = wu[0]
    wd_all[j] = wd[0]

    pl.semaphore_wait(barrier, n_exp - 1 + N_CTX - 1)

    @pl.loop(1, N_CTX)
    def _(d):
        remote(yf_all.at[c], yf_all.at[c], yf_s, yf_r, me, (c + d) % N_CTX).start()

    @pl.when(jnp.logical_not(active))
    def _():
        remote(gs_grp.at[j], gs_grp.at[j], grp_s.at[0], grp_r.at[0], me, act).start()
        remote(ys_grp.at[j], ys_grp.at[j], grp_s.at[1], grp_r.at[1], me, act).start()

    w_alls = (wg_all, wu_all, wd_all)
    j_nbr = nbr % 4

    for n, w_all in enumerate(w_alls):
        remote(w_all.at[j], w_all.at[j], w_s.at[n, 0], w_r.at[n, 0], me, nbr).start()
        remote(w_all.at[j], w_all.at[j], w_s.at[n, 1], w_r.at[n, 1], me, mate).start()

    def forward(n):
        w_all = w_alls[n]
        wait_bytes(w_all.at[j_nbr], w_r.at[n, 0])
        remote(w_all.at[j_nbr], w_all.at[j_nbr], w_s.at[n, 2], w_r.at[n, 2], me, mate).start()

    def have(n):
        w_all = w_alls[n]
        wait_bytes(w_all.at[0], w_r.at[n, 1])
        wait_bytes(w_all.at[0], w_r.at[n, 2])

    tokens = yf_ref.shape[0]

    def one_hot(hit):
        return jnp.where(hit, 1.0, 0.0).astype(BF16)

    def routes():
        expert = iota((n_exp, tokens), 0)
        named = jnp.zeros((n_exp, tokens), F32)
        gates = jnp.zeros((n_exp, tokens), F32)
        for t in range(ids_ref.shape[0]):
            hit = ids_ref[t : t + 1, :] == expert
            named = jnp.where(hit, 1.0, named)
            gates = jnp.where(hit, gate_ref[t : t + 1, :].astype(F32), gates)
        before = one_hot(iota((tokens, tokens), 0) < iota((tokens, tokens), 1))
        rank = dot_nn(named.astype(BF16), before)
        code = jnp.where(named > 0.5, rank, 255.0).astype(BF16)
        high = jnp.floor(gates * (1.0 / 256.0))
        return code, high.astype(BF16), (gates - 256.0 * high).astype(BF16)

    @pl.when(active)
    def _():
        code, _, _ = routes()
        slots = n_exp * cap
        spread = one_hot(iota((slots, n_exp), 0) // cap == iota((slots, n_exp), 1))
        place = (iota((slots, tokens), 0) % cap).astype(F32)
        chooser = one_hot(dot_nn(spread, code) == place)

        wait_bytes(yf_all.at[pl.ds(0, 7)], yf_r)
        first = wide(yf_all, 8).astype(F32)
        r = scale_of(first)
        normed = jnp.concatenate([yf_all[4 * p + i] for i in range(4)], axis=1).astype(F32)
        normed = (normed * r * g_moe[:, half]).astype(BF16)
        rows_send[...] = dot_nn(chooser, normed).astype(BF16).reshape(n_exp, cap, 512)

        @pl.loop(1, n_exp)
        def _(i):
            e = shifted(n_exp - i)
            remote(rows_send.at[e], rows_in.at[p, my_wi], disp_s.at[0], disp_r.at[0], e, c).start()

        pltpu.make_async_copy(rows_send.at[me], rows_in.at[p, my_wi], disp_r.at[0]).start()

        wait_bytes(gs_grp.at[pl.ds(0, 3)], grp_r.at[0])
        grads_send[...] = dot_nn(chooser, wide(gs_grp, 4)).astype(BF16).reshape(n_exp, cap, 512)

        @pl.loop(1, n_exp)
        def _(i):
            e = shifted(n_exp - i)
            remote(grads_send.at[e], grads_in.at[p, my_wi], disp_s.at[1], disp_r.at[1], e, c).start()

        pltpu.make_async_copy(grads_send.at[me], grads_in.at[p, my_wi], disp_r.at[1]).start()

        code, high, low = routes()
        spread = one_hot(iota((n_exp, slots), 1) // cap == iota((n_exp, slots), 0))
        place = (iota((tokens, slots), 1) % cap).astype(F32)
        taken = dot_tn(code, spread) == place
        for part, (levels, unit) in enumerate(((high, 256.0), (low, 65536.0))):
            comb[part * tokens : (part + 1) * tokens] = jnp.where(
                taken, dot_tn(levels, spread) * (1.0 / unit), 0.0
            ).astype(BF16)

    @pl.when(jnp.logical_not(active))
    def _():
        wait_bytes(yf_all.at[pl.ds(0, 7)], yf_r)

    @pl.loop(1, N_CTX)
    def _(d):
        remote(gf_all.at[c], gf_all.at[c], gf_s, gf_r, me, (c + d) % N_CTX).start()

    forward(0)
    forward(1)

    wait_bytes(rows_in.at[0], disp_r.at[0])
    remote(rows_in.at[p], rows_in.at[p], cross_s.at[0], cross_r.at[0], me, cross).start()
    forward(2)
    wait_bytes(rows_in.at[0], cross_r.at[0])
    n_rows = wins * cap
    hid = 4 * wg.shape[1]

    def both(ref):
        return jnp.concatenate([ref[0].reshape(n_rows, 512), ref[1].reshape(n_rows, 512)], axis=1)

    def weight(ref):
        return ref[...].reshape(hid, 1024)

    def weight_half(ref, cols):
        return ref[:, :, cols].reshape(hid, 512)

    have(0)
    rows = both(rows_in)
    gate_proj = dot_nt(rows, weight(wg_all))
    have(1)
    up_proj = dot_nt(rows, weight(wu_all))
    gate_keep[...] = gate_proj
    up_keep[...] = up_proj
    hidden = (gate_proj * jax.nn.sigmoid(gate_proj) * up_proj).astype(BF16)
    have(2)
    xo_send[...] = dot_nn(hidden, weight_half(wd_all, other)).astype(BF16)
    remote(xo_send, xo_recv, cross_s.at[1], cross_r.at[1], me, cross).start()
    own_out = dot_nn(hidden, weight_half(wd_all, half))

    wait_bytes(grads_in.at[0], disp_r.at[1])
    remote(grads_in.at[p], grads_in.at[p], cross_s.at[2], cross_r.at[2], me, cross).start()

    def give_back(ret, back, n):
        @pl.loop(0, wins)
        def _(i):
            wx, zi = (mx + i // zi_n) % n_x, (mz // 4 + i) % zi_n
            w = wx * n_z + (q + 4 * n_x - wx) % 4 + 4 * zi
            wi = wx * zi_n + zi

            @pl.when(w != me)
            def _():
                remote(ret.at[wi], back.at[me], ret_s.at[n], ret_r.at[n], w, c).start()

        @pl.when(active)
        def _():
            pltpu.make_async_copy(ret.at[my_wi], back.at[me], ret_r.at[n]).start()

    wait_bytes(xo_recv, cross_r.at[1])
    out_ret[...] = (own_out + xo_recv[...].astype(F32)).astype(BF16).reshape(wins, cap, 512)
    give_back(out_ret, out_back, 0)

    wait_bytes(grads_in.at[0], cross_r.at[2])
    grad_hidden = dot_nt(both(grads_in), weight(wd_all))
    gate_proj = gate_keep[...]
    sig = jax.nn.sigmoid(gate_proj)
    grad_gate = (grad_hidden * up_keep[...] * sig * (1.0 + gate_proj * (1.0 - sig))).astype(BF16)
    grad_up = (grad_hidden * gate_proj * sig).astype(BF16)
    xb_send[...] = (
        dot_nn(grad_gate, weight_half(wg_all, other)) + dot_nn(grad_up, weight_half(wu_all, other))
    ).astype(BF16)
    remote(xb_send, xb_recv, cross_s.at[3], cross_r.at[3], me, cross).start()
    own_back = dot_nn(grad_gate, weight_half(wg_all, half)) + dot_nn(grad_up, weight_half(wu_all, half))
    wait_bytes(xb_recv, cross_r.at[3])
    bk_ret[...] = (own_back + xb_recv[...].astype(F32)).astype(BF16).reshape(wins, cap, 512)
    give_back(bk_ret, bk_back, 1)

    def combined(back):
        sums = dot_nn(comb[...], back[...].reshape(n_exp * cap, 512))
        return sums[0:tokens] + sums[tokens : 2 * tokens]

    def to_all(ref, ssem, rsem):
        @pl.loop(1, N_CTX)
        def _(d):
            remote(ref.at[p], ref.at[p], ssem.at[d - 1], rsem.at[p], me, (c + d) % N_CTX).start()

    @pl.when(active)
    def _():
        wait_bytes(ys_grp.at[pl.ds(0, 3)], grp_r.at[1])
        wait_bytes(out_back, ret_r.at[0])
        sec[p] = (wide(ys_grp, 4).astype(F32) - combined(out_back)).astype(BF16)
        to_all(sec, sec_s, sec_r)

    @pl.when(jnp.logical_not(active))
    def _():
        wait_bytes(sec.at[0], sec_r.at[p])

    wait_bytes(sec.at[0], sec_r.at[1 - p])
    own_lanes = pl.ds(pl.multiple_of(j * 128, 128), 128)
    second_out[...] = sec[p, :, own_lanes]

    second = jnp.concatenate([sec[0], sec[1]], axis=1).astype(F32)
    r_second = scale_of(second)
    attn_in = (second * r_second * g_attn[...]).astype(BF16)
    queries = dot_nn(attn_in, wq[...]).astype(BF16)
    wl2 = jnp.concatenate([wl[...], wl[...]], axis=0)
    lane = iota((tokens, 128), 1)
    mine = lane // 64 == k
    lat_all[c] = jnp.where(mine, dot_nt(attn_in, wl2), 0.0).astype(BF16)

    @pl.loop(1, N_CTX)
    def _(d):
        remote(lat_all.at[c], lat_all.at[c], lat_s, lat_r, me, (c + d) % N_CTX).start()

    wait_bytes(lat_all.at[pl.ds(0, 7)], lat_r)
    latent = jnp.concatenate(
        [lat_all[2 * i].astype(F32) + lat_all[2 * i + 1].astype(F32) for i in range(4)], axis=1
    )
    r_latent = scale_of(latent)
    latent_norm = (latent * r_latent * g_lat[...]).astype(BF16)
    keys = dot_nn(latent_norm, wk[...]).astype(BF16)
    values = dot_nn(latent_norm, wv[...]).astype(BF16)
    factor = 1.0 / math.sqrt(128.0)
    bounded = jnp.tanh(dot_nt(queries, keys) * (factor / LIMIT))
    allowed = iota((tokens, tokens), 1) <= iota((tokens, tokens), 0)
    weights = jnp.where(allowed, jnp.exp(LIMIT * bounded), 0.0)
    probs = weights / jnp.sum(weights, axis=-1, keepdims=True)
    probs_low = probs.astype(BF16)
    mixed = dot_nn(probs_low, values).astype(BF16)
    attn_part = dot_nn(mixed, wo[...]).astype(BF16)
    for i in range(N_CTX):
        ao_send[i] = attn_part[:, 128 * i : 128 * i + 128]
    ao_recv[c] = ao_send[c]

    @pl.loop(1, N_CTX)
    def _(d):
        to = (c + d) % N_CTX
        remote(ao_send.at[to], ao_recv.at[c], ao_s, ao_r, me, to).start()

    @pl.when(active)
    def _():
        wait_bytes(bk_back, ret_r.at[1])
        gm[p] = combined(bk_back).astype(BF16)
        to_all(gm, gm_s, gm_r)

    wait_bytes(ao_recv.at[pl.ds(0, 7)], ao_r)
    attn_out = ao_recv[0].astype(F32)
    for i in range(1, N_CTX):
        attn_out = attn_out + ao_recv[i].astype(F32)
    first_out[...] = (yf_ref[...].astype(F32) - attn_out).astype(BF16)
    wait_bytes(gf_all.at[pl.ds(0, 7)], gf_r)

    @pl.when(jnp.logical_not(active))
    def _():
        wait_bytes(gm.at[0], gm_r.at[p])

    wait_bytes(gm.at[0], gm_r.at[1 - p])

    first = wide(yf_all, 8).astype(F32)
    r_first = scale_of(first)
    lifted = g_moe[...] * jnp.concatenate([gm[0], gm[1]], axis=1).astype(F32)
    inner = jnp.mean(lifted * first, axis=-1, keepdims=True)
    total = wide(gf_all, 8).astype(F32) + (r_first * lifted - first * (r_first * r_first * r_first) * inner)
    total = total.astype(BF16)
    for i in range(N_CTX):
        gff[i] = total[:, 128 * i : 128 * i + 128]
    gfirst_out[...] = gff[c]
    grad_mixed = dot_nt(total, wo[...]).astype(BF16)
    grad_probs = dot_nt(grad_mixed, values)
    row_delta = jnp.sum(probs * grad_probs, axis=-1, keepdims=True)
    grad_scores = (probs * (grad_probs - row_delta) * (1.0 - bounded * bounded) * factor).astype(BF16)
    grad_keys = dot_tn(grad_scores, queries).astype(BF16)
    grad_values = dot_tn(probs_low, grad_mixed).astype(BF16)
    lat_part = dot_nt(grad_keys, wk[...]) + dot_nt(grad_values, wv[...])
    stat = jnp.sum(g_lat[...] * lat_part * latent, axis=-1, keepdims=True)
    stat_high = stat.astype(BF16).astype(F32)
    stat_pair = jnp.where(lane % 2 == 0, stat_high, stat - stat_high)
    for i in range(N_CTX):
        piece = lat_part[:, 128 * (i // 2) : 128 * (i // 2) + 128]
        lg_send[i] = jnp.where(lane // 64 == i % 2, piece, stat_pair).astype(BF16)
    lg_recv[c] = lg_send[c]

    @pl.loop(1, N_CTX)
    def _(d):
        to = (c + d) % N_CTX
        remote(lg_send.at[to], lg_recv.at[c], lg_s, lg_r, me, to).start()

    grad_queries = dot_nn(grad_scores, keys).astype(BF16)
    input_part = dot_nt(grad_queries, wq[...])
    own_latent = lat_all[c].astype(F32)
    pair_gain = g_lat[:, pl.ds(pl.multiple_of((c // 2) * 128, 128), 128)]
    wait_bytes(lg_recv.at[pl.ds(0, 7)], lg_r)
    arrived = lg_recv[0].astype(F32)
    for i in range(1, N_CTX):
        arrived = arrived + lg_recv[i].astype(F32)
    lat_inner = jnp.sum(jnp.where(mine, 0.0, arrived), axis=-1, keepdims=True) * (1.0 / (32.0 * 512.0))
    grad_latent = r_latent * (pair_gain * arrived) - own_latent * (r_latent * r_latent * r_latent) * lat_inner
    grad_latent = jnp.where(mine, grad_latent, 0.0).astype(BF16)
    input_part = input_part + dot_nn(grad_latent, wl2)
    stat = jnp.sum(g_attn[...] * input_part * second, axis=-1, keepdims=True)
    stat_row = jnp.broadcast_to(stat, (tokens, 128)).T[0:8]
    stat_high = stat_row.astype(BF16).astype(F32)
    stat_rows = jnp.concatenate([stat_high, stat_row - stat_high], axis=0).astype(BF16)
    for i in range(N_CTX):
        ia_send[i, 0:tokens] = input_part[:, 128 * i : 128 * i + 128].astype(BF16)
        ia_send[i, tokens : tokens + 16] = stat_rows
    ia_recv[c] = ia_send[c]

    @pl.loop(1, N_CTX)
    def _(d):
        to = (c + d) % N_CTX
        remote(ia_send.at[to], ia_recv.at[c], ia_s, ia_r, me, to).start()

    wait_bytes(ia_recv.at[pl.ds(0, 7)], ia_r)
    arrived = ia_recv[0].astype(F32)
    for i in range(1, N_CTX):
        arrived = arrived + ia_recv[i].astype(F32)
    stat_row = arrived[tokens : tokens + 1] + arrived[tokens + 8 : tokens + 9]
    in_inner = jnp.broadcast_to(stat_row, (tokens, tokens)).T * (1.0 / 1024.0)
    own_gain = g_attn[:, pl.ds(pl.multiple_of(c * 128, 128), 128)]
    own_second = sec[p, :, own_lanes].astype(F32)
    grad_in = r_second * (own_gain * arrived[0:tokens]) - own_second * (
        r_second * r_second * r_second
    ) * in_inner
    gsecond_out[...] = (gs_ref[...].astype(F32) + grad_in).astype(BF16)

    for ref, sem in (
        (yf_all, yf_s),
        (gf_all, gf_s),
        (lat_all, lat_s),
        (ao_send, ao_s),
        (lg_send, lg_s),
        (ia_send, ia_s),
    ):
        wait_bytes(ref.at[pl.ds(0, 7)], sem)
    for n, w_all in enumerate(w_alls):
        for i in range(3):
            wait_bytes(w_all.at[0], w_s.at[n, i])
    wait_bytes(rows_in.at[0], cross_s.at[0])
    wait_bytes(xo_send, cross_s.at[1])
    wait_bytes(grads_in.at[0], cross_s.at[2])
    wait_bytes(xb_send, cross_s.at[3])

    @pl.when(active)
    def _():
        for n, ref in enumerate((rows_send, grads_send)):
            wait_bytes(ref.at[pl.ds(0, n_exp - 1)], disp_s.at[n])
        for n, ref in enumerate((out_ret, bk_ret)):
            if wins > 1:
                wait_bytes(ref.at[pl.ds(0, wins - 1)], ret_s.at[n])
        for ref, sem in ((sec, sec_s), (gm, gm_s)):
            for d in range(N_CTX - 1):
                wait_bytes(ref.at[0], sem.at[d])

    @pl.when(jnp.logical_not(active))
    def _():
        wait_bytes(gs_grp.at[0], grp_s.at[0])
        wait_bytes(ys_grp.at[0], grp_s.at[1])
        for n, ref in enumerate((out_ret, bk_ret)):
            wait_bytes(ref, ret_s.at[n])


def local(n_x, n_z, cap, *args):
    (yf, ys, gf, gs, ids, gate, ga, gl, gmo, wq, wl, wk, wv, wo, wg, wu, wd) = args
    tokens = yf.shape[0]
    n_exp = n_x * n_z
    wins = n_exp // 4
    hid = wg.shape[2]
    block = (tokens, 128)
    vmem = lambda *s: pltpu.VMEM(s, BF16)
    dma = pltpu.SemaphoreType.DMA
    one = dma(())
    out = jax.ShapeDtypeStruct(block, BF16)
    spec = pl.BlockSpec(memory_space=pltpu.VMEM)
    return pl.pallas_call(
        functools.partial(kernel, n_x, n_z, cap),
        out_shape=(out,) * 4,
        in_specs=[spec] * 17,
        out_specs=(spec,) * 4,
        scratch_shapes=[
            vmem(8, *block),
            vmem(8, *block),
            vmem(4, *block),
            vmem(4, *block),
            vmem(4, hid, 1024),
            vmem(4, hid, 1024),
            vmem(4, hid, 1024),
            vmem(2 * tokens, n_exp * cap),
            vmem(n_exp, cap, 512),
            vmem(n_exp, cap, 512),
            vmem(2, wins, cap, 512),
            vmem(2, wins, cap, 512),
            pltpu.VMEM((wins * cap, 4 * hid), F32),
            pltpu.VMEM((wins * cap, 4 * hid), F32),
            vmem(wins * cap, 512),
            vmem(wins * cap, 512),
            vmem(wins, cap, 512),
            vmem(n_exp, cap, 512),
            vmem(wins * cap, 512),
            vmem(wins * cap, 512),
            vmem(wins, cap, 512),
            vmem(n_exp, cap, 512),
            vmem(2, tokens, 512),
            vmem(2, tokens, 512),
            vmem(8, *block),
            vmem(8, *block),
            vmem(8, *block),
            vmem(8, *block),
            vmem(8, *block),
            vmem(8, *block),
            vmem(8, tokens + 16, 128),
            vmem(8, tokens + 16, 128),
            one,
            one,
            one,
            one,
            dma((2,)),
            dma((2,)),
            dma((3, 3)),
            dma((3, 3)),
            dma((2,)),
            dma((2,)),
            dma((4,)),
            dma((4,)),
            dma((2,)),
            dma((2,)),
            dma((7,)),
            dma((2,)),
            dma((7,)),
            dma((2,)),
            one,
            one,
            one,
            one,
            one,
            one,
            one,
            one,
        ],
        compiler_params=pltpu.CompilerParams(
            collective_id=0, has_side_effects=True, vmem_limit_bytes=56 * 1024 * 1024
        ),
    )(
        *(yf, ys, gf, gs, ids.T, gate.T),
        *(g.reshape(1, -1) for g in (ga, gl, gmo)),
        *(wq, wl.T, wk, wv, wo),
        *(jnp.swapaxes(w, 1, 2) for w in (wg, wu)),
        wd,
    )


def solution(mesh, n_x=4, n_z=16, cap=CAP):
    rows = P("exp", "ctx")
    placed = (
        (rows,) * 4
        + (P("exp", None),) * 2
        + (P(),) * 3
        + (P(None, "ctx"),) * 4
        + (P("ctx", None), P("exp", None, "ctx"), P("exp", None, "ctx"), P("exp", "ctx", None))
    )
    return jax.shard_map(
        functools.partial(local, n_x, n_z, cap),
        mesh=mesh,
        in_specs=placed,
        out_specs=(rows,) * 4,
        check_vma=False,
    )
```

time: 783 us -> 127 us (0.16)
  waiting for transfers between devices: 579 us -> 0 us
  Pallas kernels: 0 us -> 123 us
  blocking collectives: 71.8 us -> 0 us
  starting transfers between devices: 49.4 us -> 0 us
  other arithmetic: 22.6 us -> 0 us
  matrix products: 21.9 us -> 0 us
  local copies, waits for them, and re-layouts: 22.7 us -> 3.54 us
  between operations: 14.2 us -> 0.66 us
    all_to_all x4 -> x0, waiting for transfers between devices: 352 us -> none  [the longest x1 92.4 us: local(): lax.all_to_all(send_grads, 'exp', split_axis=0, concat_axis=0, tiled=True)]
    psum x3 -> x0, waiting for transfers between devices: 188 us -> none  [the longest x1 72.4 us: local(): lax.psum(input_part.astype(jnp.bfloat16), 'ctx').astype(jnp.float32)]
    pallas_call x0 -> x1, Pallas kernels: none -> 123 us  [local(): pl.pallas_call(functools.partial(kernel, n_x, n_z, cap), out_shape=(out,)...]
    all_gather x5 -> x0, blocking collectives: 71.8 us -> none  [the longest x1 18.4 us: local(): lax.all_gather(y_first, 'ctx', axis=1, tiled=True)]
    all_to_all x4 -> x0, starting transfers between devices: 49.1 us -> none  [the longest x1 13.9 us: local(): lax.all_to_all(send_rows, 'exp', split_axis=0, concat_axis=0, tiled=True)]
    unnamed x5 -> x0, waiting for transfers between devices: 38.3 us -> none
    dot_general x20 -> x0, matrix products: 21.9 us -> none  [the longest x1 3.39 us: local(): jnp.einsum('secf,efd->secd', hidden, w_down, preferred_element_type=jnp.f...]
    reduce_sum x8 -> x0, other arithmetic: 11.4 us -> none  [the longest x1 7.53 us: local(): grad_part = jnp.sum(weights[:, :, None] * picked_grads, axis=1)]
  transfers between devices with their start and end apart: 8 -> 0, of which waited for: 8 -> 0; matrix products, arithmetic and copies ran while one was open for 2% -> 0% of each run, Pallas kernels for 0% -> 0%
where the time goes in v1:
time: 127 us
  Pallas kernels  123 us (97%)
  local copies, waits for them, and re-layouts  3.54 us (3%)
    pallas_call x1, Pallas kernels, local(): pl.pallas_call(functools.partial(kernel, n_x, n_z, cap), out_shape=(out,)...  123 us
    unnamed x10, local copies, waits for them, and re-layouts  3.54 us

profile of v1, /device:TPU:1, one launch (start us, length us, event | category | flops | bytes accessed | tf_op | source)
XLA Modules:
  0.0 126.9 jit_solution(3151424180902965714)
XLA Ops:
  0.6 122.7 %shard_map.192 = (bf16[128,128]{1,0:T(8,128)(2,1)}, bf16[128,128]{1,0:T(8,128)(2,1)}, bf16[128,128]{1,0:T(8,128)(2,1)}, bf16[128,128]{1,0:T(8,128)(2,1)}) custom-call(bf16[128,128]{1,0:T(8,128)(2,1)} %yf_ref.1, bf16[128,128]{1,0:T(8,128)(2,1)} %ys_ref.1, bf16[128,128]{1,0:T(8,128)(2,1)} %gf_ref.1, bf16[128,128]{1,0:T(8,128)(2,1)} %gs_ref.1, ...), custom_call_target="tpu_custom_call" | custom-call | tf_op jit(solution)/shard_map/pallas_call | solution.py:546
  123.3 0.0 copy-start.2
  123.3 1.4 %copy.25 = bf16[128,128]{1,0:T(8,128)(2,1)} copy(bf16[128,128]{1,0:T(8,128)(2,1)} %get-tuple-element.8) | data formatting | bytes 65536
  124.7 0.0 copy-done.2
  124.7 0.0 copy-start.1
  124.7 0.6 copy.26
  125.3 0.2 copy-done.1
  125.5 0.0 copy-start
  125.5 0.6 copy.27
  126.1 0.2 copy-done
  126.3 0.6 copy.28
Async XLA Ops:
  123.3 1.4 %copy-start.2 = (bf16[128,128]{1,0:T(8,128)(2,1)S(1)}, bf16[128,128]{1,0:T(8,128)(2,1)}, u32[]{:S(2)}) copy-start(bf16[128,128]{1,0:T(8,128)(2,1)} %get-tuple-element.9) | copy-start | bytes 98308
  124.7 0.8 copy-start.1
  125.5 0.8 copy-start

commit v2 on v1

--- a/solution.py
+++ b/solution.py
@@ -73,6 +73,7 @@
     wg_all,
     wu_all,
     wd_all,
+    chooser,
     comb,
     rows_send,
     grads_send,
@@ -141,6 +142,7 @@
     my_wi = mx * zi_n + mz // 4
     active = q == quarter
     qm, qk = quarter // 2, quarter % 2
+    acts = [2 * (i * (3 - 2 * qm) + qm) + qk for i in range(2)]
     act = 2 * (p * (3 - 2 * qm) + qm) + qk
     half = pl.ds(pl.multiple_of(p * 512, 512), 512)
     other = pl.ds(pl.multiple_of((1 - p) * 512, 512), 512)
@@ -158,20 +160,39 @@
     def wait_bytes(ref, sem):
         pltpu.make_async_copy(ref, ref, sem).wait()
 
+    owed = {}
+
+    def owe(name, ref, sem):
+        owed[name] = functools.partial(wait_bytes, ref, sem)
+
+    def settle(*names):
+        for name in names:
+            owed.pop(name)()
+
+    inactive = jnp.logical_not(active)
+
     def shifted(i):
         a, dx = i // n_x, i % n_x
         dz = (a % 2) * ((a + 1) // 2) + (1 - a % 2) * (n_z - a // 2)
         return ((mx + dx) % n_x) * n_z + (mz + dz) % n_z
 
+    def window(i):
+        wx, zi = (mx + i // zi_n) % n_x, (mz // 4 + i) % zi_n
+        return wx * n_z + (q + 4 * n_x - wx) % 4 + 4 * zi, wx * zi_n + zi
+
     barrier = pltpu.get_barrier_semaphore()
-
-    @pl.loop(1, n_exp)
-    def _(i):
-        pl.semaphore_signal(barrier, inc=1, device_id=(shifted(i), c), device_id_type=MESH)
 
     @pl.loop(1, N_CTX)
     def _(d):
         pl.semaphore_signal(barrier, inc=1, device_id=(me, (c + d) % N_CTX), device_id_type=MESH)
+
+    @pl.loop(0, wins)
+    def _(i):
+        w, _ = window(i)
+
+        @pl.when(w != me)
+        def _():
+            pl.semaphore_signal(barrier, inc=1, device_id=(w, c), device_id_type=MESH)
 
     yf_all[c] = yf_ref[...]
     gf_all[c] = gf_ref[...]
@@ -181,16 +202,39 @@
     wu_all[j] = wu[0]
     wd_all[j] = wd[0]
 
-    pl.semaphore_wait(barrier, n_exp - 1 + N_CTX - 1)
-
-    @pl.loop(1, N_CTX)
-    def _(d):
-        remote(yf_all.at[c], yf_all.at[c], yf_s, yf_r, me, (c + d) % N_CTX).start()
-
-    @pl.when(jnp.logical_not(active))
+    @pl.when(active)
+    def _():
+        pl.semaphore_wait(barrier, n_exp - 1 + N_CTX - 1)
+
+    @pl.when(inactive)
+    def _():
+        pl.semaphore_wait(barrier, N_CTX - 1)
+
+
+    def send_first(to):
+        remote(yf_all.at[c], yf_all.at[c], yf_s, yf_r, me, to).start()
+
+    def first_here(who):
+        pl.when(who)(lambda: wait_bytes(yf_all.at[pl.ds(0, 7)], yf_r))
+
+    for to in acts:
+        pl.when(to != c)(functools.partial(send_first, to))
+    owed["first, handler"] = functools.partial(first_here, active)
+
+    @pl.when(inactive)
     def _():
         remote(gs_grp.at[j], gs_grp.at[j], grp_s.at[0], grp_r.at[0], me, act).start()
         remote(ys_grp.at[j], ys_grp.at[j], grp_s.at[1], grp_r.at[1], me, act).start()
+
+    def group_sent(ref, n):
+        pl.when(inactive)(lambda: wait_bytes(ref.at[0], grp_s.at[n]))
+
+    def group_here(ref, n):
+        pl.when(active)(lambda: wait_bytes(ref.at[pl.ds(0, 3)], grp_r.at[n]))
+
+    for n, (name, ref) in enumerate((("gs", gs_grp), ("ys", ys_grp))):
+        owed[name + " sent"] = functools.partial(group_sent, ref, n)
+        owed[name] = functools.partial(group_here, ref, n)
 
     w_alls = (wg_all, wu_all, wd_all)
     j_nbr = nbr % 4
@@ -198,18 +242,22 @@
     for n, w_all in enumerate(w_alls):
         remote(w_all.at[j], w_all.at[j], w_s.at[n, 0], w_r.at[n, 0], me, nbr).start()
         remote(w_all.at[j], w_all.at[j], w_s.at[n, 1], w_r.at[n, 1], me, mate).start()
+        for i in range(2):
+            owe(f"w{n}{i} sent", w_all.at[0], w_s.at[n, i])
+            owe(f"w{n}{i}", w_all.at[0], w_r.at[n, i])
 
     def forward(n):
         w_all = w_alls[n]
-        wait_bytes(w_all.at[j_nbr], w_r.at[n, 0])
+        settle(f"w{n}0")
         remote(w_all.at[j_nbr], w_all.at[j_nbr], w_s.at[n, 2], w_r.at[n, 2], me, mate).start()
+        owe(f"w{n}2 sent", w_all.at[0], w_s.at[n, 2])
+        owe(f"w{n}2", w_all.at[0], w_r.at[n, 2])
 
     def have(n):
-        w_all = w_alls[n]
-        wait_bytes(w_all.at[0], w_r.at[n, 1])
-        wait_bytes(w_all.at[0], w_r.at[n, 2])
+        settle(f"w{n}1", f"w{n}2")
 
     tokens = yf_ref.shape[0]
+    slots = n_exp * cap
 
     def one_hot(hit):
         return jnp.where(hit, 1.0, 0.0).astype(BF16)
@@ -231,35 +279,35 @@
     @pl.when(active)
     def _():
         code, _, _ = routes()
-        slots = n_exp * cap
         spread = one_hot(iota((slots, n_exp), 0) // cap == iota((slots, n_exp), 1))
         place = (iota((slots, tokens), 0) % cap).astype(F32)
-        chooser = one_hot(dot_nn(spread, code) == place)
-
-        wait_bytes(yf_all.at[pl.ds(0, 7)], yf_r)
-        first = wide(yf_all, 8).astype(F32)
-        r = scale_of(first)
-        normed = jnp.concatenate([yf_all[4 * p + i] for i in range(4)], axis=1).astype(F32)
-        normed = (normed * r * g_moe[:, half]).astype(BF16)
-        rows_send[...] = dot_nn(chooser, normed).astype(BF16).reshape(n_exp, cap, 512)
-
+        chooser[...] = one_hot(dot_nn(spread, code) == place)
+
+    settle("first, handler")
+
+    def dispatch(n, send, arrive):
         @pl.loop(1, n_exp)
         def _(i):
             e = shifted(n_exp - i)
-            remote(rows_send.at[e], rows_in.at[p, my_wi], disp_s.at[0], disp_r.at[0], e, c).start()
-
-        pltpu.make_async_copy(rows_send.at[me], rows_in.at[p, my_wi], disp_r.at[0]).start()
-
-        wait_bytes(gs_grp.at[pl.ds(0, 3)], grp_r.at[0])
-        grads_send[...] = dot_nn(chooser, wide(gs_grp, 4)).astype(BF16).reshape(n_exp, cap, 512)
-
-        @pl.loop(1, n_exp)
-        def _(i):
-            e = shifted(n_exp - i)
-            remote(grads_send.at[e], grads_in.at[p, my_wi], disp_s.at[1], disp_r.at[1], e, c).start()
-
-        pltpu.make_async_copy(grads_send.at[me], grads_in.at[p, my_wi], disp_r.at[1]).start()
-
+            remote(send.at[e], arrive.at[p, my_wi], disp_s.at[n], disp_r.at[n], e, c).start()
+
+        pltpu.make_async_copy(send.at[me], arrive.at[p, my_wi], disp_r.at[n]).start()
+
+    def dispatch_sent(ref, n):
+        pl.when(active)(lambda: wait_bytes(ref.at[pl.ds(0, n_exp - 1)], disp_s.at[n]))
+
+    @pl.when(active)
+    def _():
+        r = scale_of(wide(yf_all, 8).astype(F32))
+        normed = jnp.concatenate([yf_all[4 * p + i] for i in range(4)], axis=1).astype(F32)
+        normed = (normed * r * g_moe[:, half]).astype(BF16)
+        rows_send[...] = dot_nn(chooser[...], normed).astype(BF16).reshape(n_exp, cap, 512)
+        dispatch(0, rows_send, rows_in)
+
+    owed["rows sent"] = functools.partial(dispatch_sent, rows_send, 0)
+    owe("rows", rows_in.at[0], disp_r.at[0])
+    @pl.when(active)
+    def _():
         code, high, low = routes()
         spread = one_hot(iota((n_exp, slots), 1) // cap == iota((n_exp, slots), 0))
         place = (iota((tokens, slots), 1) % cap).astype(F32)
@@ -269,21 +317,37 @@
                 taken, dot_tn(levels, spread) * (1.0 / unit), 0.0
             ).astype(BF16)
 
-    @pl.when(jnp.logical_not(active))
-    def _():
-        wait_bytes(yf_all.at[pl.ds(0, 7)], yf_r)
-
     @pl.loop(1, N_CTX)
     def _(d):
-        remote(gf_all.at[c], gf_all.at[c], gf_s, gf_r, me, (c + d) % N_CTX).start()
-
-    forward(0)
-    forward(1)
-
-    wait_bytes(rows_in.at[0], disp_r.at[0])
-    remote(rows_in.at[p], rows_in.at[p], cross_s.at[0], cross_r.at[0], me, cross).start()
-    forward(2)
-    wait_bytes(rows_in.at[0], cross_r.at[0])
+        to = (c + d) % N_CTX
+        pl.when((to != acts[0]) & (to != acts[1]))(functools.partial(send_first, to))
+        remote(gf_all.at[c], gf_all.at[c], gf_s, gf_r, me, to).start()
+
+    owe("first sent", yf_all.at[pl.ds(0, 7)], yf_s)
+    owed["first"] = functools.partial(first_here, inactive)
+    owe("gf sent", gf_all.at[pl.ds(0, 7)], gf_s)
+    owe("gf", gf_all.at[pl.ds(0, 7)], gf_r)
+    settle("rows")
+
+    def to_cross(n, src, dst):
+        remote(src, dst, cross_s.at[n], cross_r.at[n], me, cross).start()
+        owe(f"cross{n} sent", src, cross_s.at[n])
+        owe(f"cross{n}", dst, cross_r.at[n])
+
+    to_cross(0, rows_in.at[p], rows_in.at[p])
+    settle("gs")
+
+    @pl.when(active)
+    def _():
+        grads_send[...] = dot_nn(chooser[...], wide(gs_grp, 4)).astype(BF16).reshape(n_exp, cap, 512)
+        dispatch(1, grads_send, grads_in)
+
+    owed["grads sent"] = functools.partial(dispatch_sent, grads_send, 1)
+    owe("grads", grads_in.at[0], disp_r.at[1])
+
+    for n in range(3):
+        forward(n)
+    settle("cross0")
     n_rows = wins * cap
     hid = 4 * wg.shape[1]
 
@@ -306,18 +370,16 @@
     hidden = (gate_proj * jax.nn.sigmoid(gate_proj) * up_proj).astype(BF16)
     have(2)
     xo_send[...] = dot_nn(hidden, weight_half(wd_all, other)).astype(BF16)
-    remote(xo_send, xo_recv, cross_s.at[1], cross_r.at[1], me, cross).start()
+    to_cross(1, xo_send, xo_recv)
     own_out = dot_nn(hidden, weight_half(wd_all, half))
 
-    wait_bytes(grads_in.at[0], disp_r.at[1])
-    remote(grads_in.at[p], grads_in.at[p], cross_s.at[2], cross_r.at[2], me, cross).start()
+    settle("grads")
+    to_cross(2, grads_in.at[p], grads_in.at[p])
 
     def give_back(ret, back, n):
         @pl.loop(0, wins)
         def _(i):
-            wx, zi = (mx + i // zi_n) % n_x, (mz // 4 + i) % zi_n
-            w = wx * n_z + (q + 4 * n_x - wx) % 4 + 4 * zi
-            wi = wx * zi_n + zi
+            w, wi = window(i)
 
             @pl.when(w != me)
             def _():
@@ -327,11 +389,19 @@
         def _():
             pltpu.make_async_copy(ret.at[my_wi], back.at[me], ret_r.at[n]).start()
 
-    wait_bytes(xo_recv, cross_r.at[1])
+        def sent():
+            pl.when(inactive)(lambda: wait_bytes(ret, ret_s.at[n]))
+            if wins > 1:
+                pl.when(active)(lambda: wait_bytes(ret.at[pl.ds(0, wins - 1)], ret_s.at[n]))
+
+        owed[f"ret{n} sent"] = sent
+        owed[f"ret{n}"] = lambda: pl.when(active)(lambda: wait_bytes(back, ret_r.at[n]))
+
+    settle("cross1")
     out_ret[...] = (own_out + xo_recv[...].astype(F32)).astype(BF16).reshape(wins, cap, 512)
     give_back(out_ret, out_back, 0)
 
-    wait_bytes(grads_in.at[0], cross_r.at[2])
+    settle("cross2")
     grad_hidden = dot_nt(both(grads_in), weight(wd_all))
     gate_proj = gate_keep[...]
     sig = jax.nn.sigmoid(gate_proj)
@@ -340,9 +410,9 @@
     xb_send[...] = (
         dot_nn(grad_gate, weight_half(wg_all, other)) + dot_nn(grad_up, weight_half(wu_all, other))
     ).astype(BF16)
-    remote(xb_send, xb_recv, cross_s.at[3], cross_r.at[3], me, cross).start()
+    to_cross(3, xb_send, xb_recv)
     own_back = dot_nn(grad_gate, weight_half(wg_all, half)) + dot_nn(grad_up, weight_half(wu_all, half))
-    wait_bytes(xb_recv, cross_r.at[3])
+    settle("cross3")
     bk_ret[...] = (own_back + xb_recv[...].astype(F32)).astype(BF16).reshape(wins, cap, 512)
     give_back(bk_ret, bk_back, 1)
 
@@ -350,23 +420,31 @@
         sums = dot_nn(comb[...], back[...].reshape(n_exp * cap, 512))
         return sums[0:tokens] + sums[tokens : 2 * tokens]
 
-    def to_all(ref, ssem, rsem):
-        @pl.loop(1, N_CTX)
-        def _(d):
-            remote(ref.at[p], ref.at[p], ssem.at[d - 1], rsem.at[p], me, (c + d) % N_CTX).start()
+    def to_all(name, ref, ssem, rsem):
+        @pl.when(active)
+        def _():
+            @pl.loop(1, N_CTX)
+            def _(d):
+                remote(ref.at[p], ref.at[p], ssem, rsem.at[p], me, (c + d) % N_CTX).start()
+
+        def sent():
+            pl.when(active)(lambda: wait_bytes(ref.at[pl.ds(0, 7)], ssem))
+
+        def here():
+            pl.when(inactive)(lambda: wait_bytes(ref.at[0], rsem.at[p]))
+            wait_bytes(ref.at[0], rsem.at[1 - p])
+
+        owed[name + " sent"] = sent
+        owed[name] = here
+
+    settle("ys", "ret0")
 
     @pl.when(active)
     def _():
-        wait_bytes(ys_grp.at[pl.ds(0, 3)], grp_r.at[1])
-        wait_bytes(out_back, ret_r.at[0])
         sec[p] = (wide(ys_grp, 4).astype(F32) - combined(out_back)).astype(BF16)
-        to_all(sec, sec_s, sec_r)
-
-    @pl.when(jnp.logical_not(active))
-    def _():
-        wait_bytes(sec.at[0], sec_r.at[p])
-
-    wait_bytes(sec.at[0], sec_r.at[1 - p])
+
+    to_all("sec", sec, sec_s, sec_r)
+    settle("sec")
     own_lanes = pl.ds(pl.multiple_of(j * 128, 128), 128)
     second_out[...] = sec[p, :, own_lanes]
 
@@ -383,7 +461,9 @@
     def _(d):
         remote(lat_all.at[c], lat_all.at[c], lat_s, lat_r, me, (c + d) % N_CTX).start()
 
-    wait_bytes(lat_all.at[pl.ds(0, 7)], lat_r)
+    owe("lat sent", lat_all.at[pl.ds(0, 7)], lat_s)
+    owe("lat", lat_all.at[pl.ds(0, 7)], lat_r)
+    settle("lat")
     latent = jnp.concatenate(
         [lat_all[2 * i].astype(F32) + lat_all[2 * i + 1].astype(F32) for i in range(4)], axis=1
     )
@@ -408,24 +488,21 @@
         to = (c + d) % N_CTX
         remote(ao_send.at[to], ao_recv.at[c], ao_s, ao_r, me, to).start()
 
+    settle("ret1")
+
     @pl.when(active)
     def _():
-        wait_bytes(bk_back, ret_r.at[1])
         gm[p] = combined(bk_back).astype(BF16)
-        to_all(gm, gm_s, gm_r)
-
-    wait_bytes(ao_recv.at[pl.ds(0, 7)], ao_r)
+
+    to_all("gm", gm, gm_s, gm_r)
+    owe("ao sent", ao_recv.at[pl.ds(0, 7)], ao_s)
+    owe("ao", ao_recv.at[pl.ds(0, 7)], ao_r)
+    settle("ao")
     attn_out = ao_recv[0].astype(F32)
     for i in range(1, N_CTX):
         attn_out = attn_out + ao_recv[i].astype(F32)
     first_out[...] = (yf_ref[...].astype(F32) - attn_out).astype(BF16)
-    wait_bytes(gf_all.at[pl.ds(0, 7)], gf_r)
-
-    @pl.when(jnp.logical_not(active))
-    def _():
-        wait_bytes(gm.at[0], gm_r.at[p])
-
-    wait_bytes(gm.at[0], gm_r.at[1 - p])
+    settle("first", "gf", "gm")
 
     first = wide(yf_all, 8).astype(F32)
     r_first = scale_of(first)
@@ -460,7 +537,9 @@
     input_part = dot_nt(grad_queries, wq[...])
     own_latent = lat_all[c].astype(F32)
     pair_gain = g_lat[:, pl.ds(pl.multiple_of((c // 2) * 128, 128), 128)]
-    wait_bytes(lg_recv.at[pl.ds(0, 7)], lg_r)
+    owe("lg sent", lg_recv.at[pl.ds(0, 7)], lg_s)
+    owe("lg", lg_recv.at[pl.ds(0, 7)], lg_r)
+    settle("lg")
     arrived = lg_recv[0].astype(F32)
     for i in range(1, N_CTX):
         arrived = arrived + lg_recv[i].astype(F32)
@@ -482,7 +561,9 @@
         to = (c + d) % N_CTX
         remote(ia_send.at[to], ia_recv.at[c], ia_s, ia_r, me, to).start()
 
-    wait_bytes(ia_recv.at[pl.ds(0, 7)], ia_r)
+    owe("ia sent", ia_recv.at[pl.ds(0, 7)], ia_s)
+    owe("ia", ia_recv.at[pl.ds(0, 7)], ia_r)
+    settle("ia")
     arrived = ia_recv[0].astype(F32)
     for i in range(1, N_CTX):
         arrived = arrived + ia_recv[i].astype(F32)
@@ -495,40 +576,16 @@
     ) * in_inner
     gsecond_out[...] = (gs_ref[...].astype(F32) + grad_in).astype(BF16)
 
-    for ref, sem in (
-        (yf_all, yf_s),
-        (gf_all, gf_s),
-        (lat_all, lat_s),
-        (ao_send, ao_s),
-        (lg_send, lg_s),
-        (ia_send, ia_s),
-    ):
-        wait_bytes(ref.at[pl.ds(0, 7)], sem)
-    for n, w_all in enumerate(w_alls):
-        for i in range(3):
-            wait_bytes(w_all.at[0], w_s.at[n, i])
-    wait_bytes(rows_in.at[0], cross_s.at[0])
-    wait_bytes(xo_send, cross_s.at[1])
-    wait_bytes(grads_in.at[0], cross_s.at[2])
-    wait_bytes(xb_send, cross_s.at[3])
-
-    @pl.when(active)
-    def _():
-        for n, ref in enumerate((rows_send, grads_send)):
-            wait_bytes(ref.at[pl.ds(0, n_exp - 1)], disp_s.at[n])
-        for n, ref in enumerate((out_ret, bk_ret)):
-            if wins > 1:
-                wait_bytes(ref.at[pl.ds(0, wins - 1)], ret_s.at[n])
-        for ref, sem in ((sec, sec_s), (gm, gm_s)):
-            for d in range(N_CTX - 1):
-                wait_bytes(ref.at[0], sem.at[d])
-
-    @pl.when(jnp.logical_not(active))
-    def _():
-        wait_bytes(gs_grp.at[0], grp_s.at[0])
-        wait_bytes(ys_grp.at[0], grp_s.at[1])
-        for n, ref in enumerate((out_ret, bk_ret)):
-            wait_bytes(ref, ret_s.at[n])
+    settle(*owed)
+
+
+def hand_over(*refs):
+    sems = refs[8]
+    copies = [pltpu.make_async_copy(refs[i], refs[4 + i], sems.at[i]) for i in range(4)]
+    for copy in copies:
+        copy.start()
+    for copy in copies:
+        copy.wait()
 
 
 def local(n_x, n_z, cap, *args):
@@ -543,7 +600,7 @@
     one = dma(())
     out = jax.ShapeDtypeStruct(block, BF16)
     spec = pl.BlockSpec(memory_space=pltpu.VMEM)
-    return pl.pallas_call(
+    results = pl.pallas_call(
         functools.partial(kernel, n_x, n_z, cap),
         out_shape=(out,) * 4,
         in_specs=[spec] * 17,
@@ -556,6 +613,7 @@
             vmem(4, hid, 1024),
             vmem(4, hid, 1024),
             vmem(4, hid, 1024),
+            vmem(n_exp * cap, tokens),
             vmem(2 * tokens, n_exp * cap),
             vmem(n_exp, cap, 512),
             vmem(n_exp, cap, 512),
@@ -571,8 +629,8 @@
             vmem(wins * cap, 512),
             vmem(wins, cap, 512),
             vmem(n_exp, cap, 512),
-            vmem(2, tokens, 512),
-            vmem(2, tokens, 512),
+            vmem(8, tokens, 512),
+            vmem(8, tokens, 512),
             vmem(8, *block),
             vmem(8, *block),
             vmem(8, *block),
@@ -595,9 +653,9 @@
             dma((4,)),
             dma((2,)),
             dma((2,)),
-            dma((7,)),
+            one,
             dma((2,)),
-            dma((7,)),
+            one,
             dma((2,)),
             one,
             one,
@@ -618,6 +676,14 @@
         *(jnp.swapaxes(w, 1, 2) for w in (wg, wu)),
         wd,
     )
+    place = pl.BlockSpec(memory_space=pl.ANY)
+    return pl.pallas_call(
+        hand_over,
+        out_shape=(out,) * 4,
+        in_specs=[place] * 4,
+        out_specs=(place,) * 4,
+        scratch_shapes=[dma((4,))],
+    )(*results)
 
 
 def solution(mesh, n_x=4, n_z=16, cap=CAP):

time: 127 us -> 119 us (0.937)
  Pallas kernels: 123 us -> 118 us
  local copies, waits for them, and re-layouts: 3.54 us -> 0 us
    pallas_call x1, Pallas kernels: 123 us -> 113 us  [local(): pl.pallas_call(functools.partial(kernel, n_x, n_z, cap), out_shape=(out,)...]
    pallas_call x0 -> x1, Pallas kernels: none -> 5.11 us  [local(): pl.pallas_call(hand_over, out_shape=(out,) * 4, in_specs=[place] * 4, out...]
    unnamed x10 -> x0, local copies, waits for them, and re-layouts: 3.54 us -> none
where the time goes in v2:
time: 119 us; the launch traced here: 118 us
  Pallas kernels  118 us (99%)
    pallas_call x1, Pallas kernels, local(): pl.pallas_call(functools.partial(kernel, n_x, n_z, cap), out_shape=(out,)...  113 us
    pallas_call x1, Pallas kernels, local(): pl.pallas_call(hand_over, out_shape=(out,) * 4, in_specs=[place] * 4, out...  5.11 us

profile of v2, /device:TPU:1, one launch (start us, length us, event | category | flops | bytes accessed | tf_op | source)
XLA Modules:
  0.0 118.4 jit_solution(3029680680505788253)
XLA Ops:
  0.6 112.6 %shard_map.192 = (bf16[128,128]{1,0:T(8,128)(2,1)}, bf16[128,128]{1,0:T(8,128)(2,1)}, bf16[128,128]{1,0:T(8,128)(2,1)}, bf16[128,128]{1,0:T(8,128)(2,1)}) custom-call(bf16[128,128]{1,0:T(8,128)(2,1)} %yf_ref.1, bf16[128,128]{1,0:T(8,128)(2,1)} %ys_ref.1, bf16[128,128]{1,0:T(8,128)(2,1)} %gf_ref.1, bf16[128,128]{1,0:T(8,128)(2,1)} %gs_ref.1, ...), custom_call_target="tpu_custom_call" | custom-call | tf_op jit(solution)/shard_map/pallas_call | solution.py:603
  113.3 5.1 %shard_map.193 = (bf16[128,128]{1,0:T(8,128)(2,1)}, bf16[128,128]{1,0:T(8,128)(2,1)}, bf16[128,128]{1,0:T(8,128)(2,1)}, bf16[128,128]{1,0:T(8,128)(2,1)}) custom-call(bf16[128,128]{1,0:T(8,128)(2,1)} %get-tuple-element.8.refs_0_, bf16[128,128]{1,0:T(8,128)(2,1)} %get-tuple-element.9.refs_1_, bf16[128,128]{1,0:T(8,128)(2,1)} %get-tuple-element.10.refs_2_, ...), custom_call_target="tpu_custom_call" | custom-call | tf_op jit(solution)/shard_map/pallas_call | solution.py:680

commit v3 on v2

--- a/solution.py
+++ b/solution.py
@@ -90,13 +90,16 @@
     bk_ret,
     bk_back,
     sec,
-    gm,
+    wo_split,
+    wo_all,
+    gp_send,
+    gp_recv,
+    us,
+    us_in,
     lat_all,
     ao_send,
     ao_recv,
-    gff,
-    lg_send,
-    lg_recv,
+    wl_all,
     ia_send,
     ia_recv,
     yf_s,
@@ -115,14 +118,18 @@
     ret_r,
     sec_s,
     sec_r,
-    gm_s,
-    gm_r,
+    wo_s,
+    wo_r,
+    gp_s,
+    gp_r,
+    us_s,
+    us_r,
     lat_s,
     lat_r,
     ao_s,
     ao_r,
-    lg_s,
-    lg_r,
+    wl_s,
+    wl_r,
     ia_s,
     ia_r,
 ):
@@ -177,7 +184,7 @@
         return ((mx + dx) % n_x) * n_z + (mz + dz) % n_z
 
     def window(i):
-        wx, zi = (mx + i // zi_n) % n_x, (mz // 4 + i) % zi_n
+        wx, zi = (mx + i % n_x) % n_x, (mz // 4 + 2 + i // n_x) % zi_n
         return wx * n_z + (q + 4 * n_x - wx) % 4 + 4 * zi, wx * zi_n + zi
 
     barrier = pltpu.get_barrier_semaphore()
@@ -201,6 +208,7 @@
     wg_all[j] = wg[0]
     wu_all[j] = wu[0]
     wd_all[j] = wd[0]
+    wl_all[c] = wl[...]
 
     @pl.when(active)
     def _():
@@ -246,6 +254,15 @@
             owe(f"w{n}{i} sent", w_all.at[0], w_s.at[n, i])
             owe(f"w{n}{i}", w_all.at[0], w_r.at[n, i])
 
+    @pl.loop(1, 4)
+    def _(d):
+        remote(wl_all.at[c], wl_all.at[c], wl_s.at[0], wl_r.at[0], me, (c + 2 * d) % N_CTX).start()
+
+    remote(wl_all.at[c], wl_all.at[c], wl_s.at[0], wl_r.at[1], me, mate).start()
+    owe("wl sent", wl_all.at[pl.ds(0, 4)], wl_s.at[0])
+    owe("wl, far", wl_all.at[pl.ds(0, 3)], wl_r.at[0])
+    owe("wl, mate", wl_all.at[0], wl_r.at[1])
+
     def forward(n):
         w_all = w_alls[n]
         settle(f"w{n}0")
@@ -258,6 +275,15 @@
 
     tokens = yf_ref.shape[0]
     slots = n_exp * cap
+
+    def stat_rows(stat):
+        row = jnp.broadcast_to(stat, (tokens, 128)).T[0:8]
+        high = row.astype(BF16).astype(F32)
+        return jnp.concatenate([high, row - high], axis=0).astype(BF16)
+
+    def stat_column(arrived, at):
+        row = arrived[at : at + 1] + arrived[at + 8 : at + 9]
+        return jnp.broadcast_to(row, (tokens, tokens)).T
 
     def one_hot(hit):
         return jnp.where(hit, 1.0, 0.0).astype(BF16)
@@ -347,6 +373,16 @@
 
     for n in range(3):
         forward(n)
+    settle("wl, far")
+
+    @pl.loop(1, 4)
+    def _(d):
+        slot = (c + 2 * d) % N_CTX
+        remote(wl_all.at[slot], wl_all.at[slot], wl_s.at[1], wl_r.at[2], me, mate).start()
+
+    owe("wl forwarded", wl_all.at[pl.ds(0, 3)], wl_s.at[1])
+    owe("wl, mate's far", wl_all.at[pl.ds(0, 3)], wl_r.at[2])
+
     settle("cross0")
     n_rows = wins * cap
     hid = 4 * wg.shape[1]
@@ -401,6 +437,21 @@
     out_ret[...] = (own_out + xo_recv[...].astype(F32)).astype(BF16).reshape(wins, cap, 512)
     give_back(out_ret, out_back, 0)
 
+    for i in range(2):
+        wo_split[i] = wo[:, 512 * i : 512 * i + 512]
+    wo_all[c] = wo_split[p]
+
+    def send_wo(i):
+        remote(wo_split.at[i], wo_all.at[c], wo_s, wo_r, me, acts[i]).start()
+
+    def wo_sent():
+        pl.when(inactive)(lambda: wait_bytes(wo_split, wo_s))
+        pl.when(active)(lambda: wait_bytes(wo_split.at[0], wo_s))
+
+    for i in range(2):
+        pl.when(acts[i] != c)(functools.partial(send_wo, i))
+    owed["wo sent"] = wo_sent
+    owed["wo"] = lambda: pl.when(active)(lambda: wait_bytes(wo_all.at[pl.ds(0, 7)], wo_r))
     settle("cross2")
     grad_hidden = dot_nt(both(grads_in), weight(wd_all))
     gate_proj = gate_keep[...]
@@ -415,7 +466,6 @@
     settle("cross3")
     bk_ret[...] = (own_back + xb_recv[...].astype(F32)).astype(BF16).reshape(wins, cap, 512)
     give_back(bk_ret, bk_back, 1)
-
     def combined(back):
         sums = dot_nn(comb[...], back[...].reshape(n_exp * cap, 512))
         return sums[0:tokens] + sums[tokens : 2 * tokens]
@@ -488,72 +538,89 @@
         to = (c + d) % N_CTX
         remote(ao_send.at[to], ao_recv.at[c], ao_s, ao_r, me, to).start()
 
-    settle("ret1")
-
-    @pl.when(active)
-    def _():
-        gm[p] = combined(bk_back).astype(BF16)
-
-    to_all("gm", gm, gm_s, gm_r)
     owe("ao sent", ao_recv.at[pl.ds(0, 7)], ao_s)
     owe("ao", ao_recv.at[pl.ds(0, 7)], ao_r)
+    settle("first", "gf")
+    first = wide(yf_all, 8).astype(F32)
+    r_first = scale_of(first)
+    turned = dot_nt((first * (r_first * r_first * r_first)).astype(BF16), wo[...])
+
+    settle("wl, mate", "wl, mate's far")
+    own_cols = pl.ds(pl.multiple_of(c * 128, 128), 128)
+    latent_cube = (latent * (r_latent * r_latent * r_latent)).astype(BF16)
+    project = wl_all[...].reshape(512, 1024)
+    own_turn = dot_nn(latent_cube, wl_all[:, :, own_cols].reshape(512, 128))
+    turn_stat = jnp.sum(g_attn[...] * dot_nn(latent_cube, project) * second, axis=-1, keepdims=True)
+
+    settle("ret1", "wo")
+
+    @pl.when(active)
+    def _():
+        grad = combined(bk_back)
+        lifted = g_moe[:, half] * grad
+        own_first = jnp.concatenate([yf_all[4 * p + i] for i in range(4)], axis=1).astype(F32)
+        own_grad = jnp.concatenate([gf_all[4 * p + i] for i in range(4)], axis=1).astype(F32)
+        part = dot_nt((own_grad + r_first * lifted).astype(BF16), wo_all[...].reshape(1024, 512))
+        inner_rows = stat_rows(jnp.sum(lifted * own_first, axis=-1, keepdims=True))
+        for i in range(N_CTX):
+            gp_send[i, 0:tokens] = part[:, 128 * i : 128 * i + 128].astype(BF16)
+            gp_send[i, tokens : tokens + 16] = inner_rows
+        gp_recv[p] = gp_send[c]
+
+        @pl.loop(1, N_CTX)
+        def _(d):
+            to = (c + d) % N_CTX
+            remote(gp_send.at[to], gp_recv.at[p], gp_s, gp_r.at[p], me, to).start()
+
+        for i in range(4):
+            us[i] = grad[:, 128 * i : 128 * i + 128].astype(BF16)
+        us_in[...] = us[j]
+
+        @pl.loop(1, 4)
+        def _(d):
+            to = (j + d) % 4
+            remote(us.at[to], us_in, us_s, us_r, me, 4 * p + to).start()
+
+    def parts_sent():
+        @pl.when(active)
+        def _():
+            wait_bytes(gp_send.at[pl.ds(0, 7)], gp_s)
+            wait_bytes(us.at[pl.ds(0, 3)], us_s)
+
+    def parts_here():
+        pl.when(inactive)(lambda: wait_bytes(gp_recv.at[0], gp_r.at[p]))
+        wait_bytes(gp_recv.at[0], gp_r.at[1 - p])
+
+    owed["parts sent"] = parts_sent
+    owed["parts"] = parts_here
+    owed["us"] = lambda: pl.when(inactive)(lambda: wait_bytes(us_in, us_r))
+
     settle("ao")
     attn_out = ao_recv[0].astype(F32)
     for i in range(1, N_CTX):
         attn_out = attn_out + ao_recv[i].astype(F32)
     first_out[...] = (yf_ref[...].astype(F32) - attn_out).astype(BF16)
-    settle("first", "gf", "gm")
-
-    first = wide(yf_all, 8).astype(F32)
-    r_first = scale_of(first)
-    lifted = g_moe[...] * jnp.concatenate([gm[0], gm[1]], axis=1).astype(F32)
-    inner = jnp.mean(lifted * first, axis=-1, keepdims=True)
-    total = wide(gf_all, 8).astype(F32) + (r_first * lifted - first * (r_first * r_first * r_first) * inner)
-    total = total.astype(BF16)
-    for i in range(N_CTX):
-        gff[i] = total[:, 128 * i : 128 * i + 128]
-    gfirst_out[...] = gff[c]
-    grad_mixed = dot_nt(total, wo[...]).astype(BF16)
+
+    settle("parts")
+    arrived = gp_recv[0].astype(F32) + gp_recv[1].astype(F32)
+    first_inner = stat_column(arrived, tokens) * (1.0 / 1024.0)
+    grad_mixed = (arrived[0:tokens] - first_inner * turned).astype(BF16)
     grad_probs = dot_nt(grad_mixed, values)
     row_delta = jnp.sum(probs * grad_probs, axis=-1, keepdims=True)
     grad_scores = (probs * (grad_probs - row_delta) * (1.0 - bounded * bounded) * factor).astype(BF16)
     grad_keys = dot_tn(grad_scores, queries).astype(BF16)
     grad_values = dot_tn(probs_low, grad_mixed).astype(BF16)
     lat_part = dot_nt(grad_keys, wk[...]) + dot_nt(grad_values, wv[...])
-    stat = jnp.sum(g_lat[...] * lat_part * latent, axis=-1, keepdims=True)
-    stat_high = stat.astype(BF16).astype(F32)
-    stat_pair = jnp.where(lane % 2 == 0, stat_high, stat - stat_high)
-    for i in range(N_CTX):
-        piece = lat_part[:, 128 * (i // 2) : 128 * (i // 2) + 128]
-        lg_send[i] = jnp.where(lane // 64 == i % 2, piece, stat_pair).astype(BF16)
-    lg_recv[c] = lg_send[c]
-
-    @pl.loop(1, N_CTX)
-    def _(d):
-        to = (c + d) % N_CTX
-        remote(lg_send.at[to], lg_recv.at[c], lg_s, lg_r, me, to).start()
-
+    lifted = g_lat[...] * lat_part
     grad_queries = dot_nn(grad_scores, keys).astype(BF16)
-    input_part = dot_nt(grad_queries, wq[...])
-    own_latent = lat_all[c].astype(F32)
-    pair_gain = g_lat[:, pl.ds(pl.multiple_of((c // 2) * 128, 128), 128)]
-    owe("lg sent", lg_recv.at[pl.ds(0, 7)], lg_s)
-    owe("lg", lg_recv.at[pl.ds(0, 7)], lg_r)
-    settle("lg")
-    arrived = lg_recv[0].astype(F32)
-    for i in range(1, N_CTX):
-        arrived = arrived + lg_recv[i].astype(F32)
-    lat_inner = jnp.sum(jnp.where(mine, 0.0, arrived), axis=-1, keepdims=True) * (1.0 / (32.0 * 512.0))
-    grad_latent = r_latent * (pair_gain * arrived) - own_latent * (r_latent * r_latent * r_latent) * lat_inner
-    grad_latent = jnp.where(mine, grad_latent, 0.0).astype(BF16)
-    input_part = input_part + dot_nn(grad_latent, wl2)
+    input_part = dot_nt(grad_queries, wq[...]) + dot_nn((r_latent * lifted).astype(BF16), project)
+    lat_stat = stat_rows(jnp.sum(lifted * latent, axis=-1, keepdims=True))
     stat = jnp.sum(g_attn[...] * input_part * second, axis=-1, keepdims=True)
-    stat_row = jnp.broadcast_to(stat, (tokens, 128)).T[0:8]
-    stat_high = stat_row.astype(BF16).astype(F32)
-    stat_rows = jnp.concatenate([stat_high, stat_row - stat_high], axis=0).astype(BF16)
+    in_stat = stat_rows(stat)
     for i in range(N_CTX):
         ia_send[i, 0:tokens] = input_part[:, 128 * i : 128 * i + 128].astype(BF16)
-        ia_send[i, tokens : tokens + 16] = stat_rows
+        ia_send[i, tokens : tokens + 16] = in_stat
+        ia_send[i, tokens + 16 : tokens + 32] = lat_stat
     ia_recv[c] = ia_send[c]
 
     @pl.loop(1, N_CTX)
@@ -561,17 +628,23 @@
         to = (c + d) % N_CTX
         remote(ia_send.at[to], ia_recv.at[c], ia_s, ia_r, me, to).start()
 
+    settle("us")
+    moe_gain = g_moe[:, own_cols]
+    grad_first = r_first * (moe_gain * us_in[...].astype(F32)) - yf_ref[...].astype(F32) * (
+        r_first * r_first * r_first
+    ) * first_inner
+    gfirst_out[...] = (gf_ref[...].astype(F32) + grad_first).astype(BF16)
     owe("ia sent", ia_recv.at[pl.ds(0, 7)], ia_s)
     owe("ia", ia_recv.at[pl.ds(0, 7)], ia_r)
     settle("ia")
     arrived = ia_recv[0].astype(F32)
     for i in range(1, N_CTX):
         arrived = arrived + ia_recv[i].astype(F32)
-    stat_row = arrived[tokens : tokens + 1] + arrived[tokens + 8 : tokens + 9]
-    in_inner = jnp.broadcast_to(stat_row, (tokens, tokens)).T * (1.0 / 1024.0)
-    own_gain = g_attn[:, pl.ds(pl.multiple_of(c * 128, 128), 128)]
+    lat_inner = stat_column(arrived, tokens + 16) * (1.0 / 512.0)
+    in_inner = (stat_column(arrived, tokens) - lat_inner * turn_stat) * (1.0 / 1024.0)
+    own_gain = g_attn[:, own_cols]
     own_second = sec[p, :, own_lanes].astype(F32)
-    grad_in = r_second * (own_gain * arrived[0:tokens]) - own_second * (
+    grad_in = r_second * (own_gain * (arrived[0:tokens] - lat_inner * own_turn)) - own_second * (
         r_second * r_second * r_second
     ) * in_inner
     gsecond_out[...] = (gs_ref[...].astype(F32) + grad_in).astype(BF16)
@@ -580,12 +653,8 @@
 
 
 def hand_over(*refs):
-    sems = refs[8]
-    copies = [pltpu.make_async_copy(refs[i], refs[4 + i], sems.at[i]) for i in range(4)]
-    for copy in copies:
-        copy.start()
-    for copy in copies:
-        copy.wait()
+    for i in range(4):
+        refs[4 + i][...] = refs[i][...]
 
 
 def local(n_x, n_z, cap, *args):
@@ -630,15 +699,18 @@
             vmem(wins, cap, 512),
             vmem(n_exp, cap, 512),
             vmem(8, tokens, 512),
-            vmem(8, tokens, 512),
+            vmem(2, 128, 512),
+            vmem(8, 128, 512),
+            vmem(8, tokens + 16, 128),
+            vmem(2, tokens + 16, 128),
+            vmem(4, *block),
+            vmem(*block),
             vmem(8, *block),
             vmem(8, *block),
             vmem(8, *block),
-            vmem(8, *block),
-            vmem(8, *block),
-            vmem(8, *block),
-            vmem(8, tokens + 16, 128),
-            vmem(8, tokens + 16, 128),
+            vmem(8, 64, 1024),
+            vmem(8, tokens + 32, 128),
+            vmem(8, tokens + 32, 128),
             one,
             one,
             one,
@@ -656,13 +728,17 @@
             one,
             dma((2,)),
             one,
-            dma((2,)),
-            one,
-            one,
-            one,
-            one,
-            one,
-            one,
+            one,
+            one,
+            dma((2,)),
+            one,
+            one,
+            one,
+            one,
+            one,
+            one,
+            dma((2,)),
+            dma((3,)),
             one,
             one,
         ],
@@ -676,13 +752,8 @@
         *(jnp.swapaxes(w, 1, 2) for w in (wg, wu)),
         wd,
     )
-    place = pl.BlockSpec(memory_space=pl.ANY)
     return pl.pallas_call(
-        hand_over,
-        out_shape=(out,) * 4,
-        in_specs=[place] * 4,
-        out_specs=(place,) * 4,
-        scratch_shapes=[dma((4,))],
+        hand_over, out_shape=(out,) * 4, in_specs=[spec] * 4, out_specs=(spec,) * 4
     )(*results)
 
 

time: 119 us -> 112 us (0.941)
  Pallas kernels: 118 us -> 111 us
    pallas_call x1, Pallas kernels: 5.11 us -> 1.46 us  [local(): pl.pallas_call(hand_over, out_shape=(out,) * 4, in_specs=[spec] * 4, out_...]
    pallas_call x1, Pallas kernels: 113 us -> 110 us  [local(): pl.pallas_call(functools.partial(kernel, n_x, n_z, cap), out_shape=(out,)...]
where the time goes in v3:
time: 112 us
  Pallas kernels  111 us (99%)
    pallas_call x1, Pallas kernels, local(): pl.pallas_call(functools.partial(kernel, n_x, n_z, cap), out_shape=(out,)...  110 us

profile of v3, /device:TPU:1, one launch (start us, length us, event | category | flops | bytes accessed | tf_op | source)
XLA Modules:
  0.0 112.1 jit_solution(14630040718679734707)
XLA Ops:
  0.6 109.9 %shard_map.192 = (bf16[128,128]{1,0:T(8,128)(2,1)}, bf16[128,128]{1,0:T(8,128)(2,1)}, bf16[128,128]{1,0:T(8,128)(2,1)}, bf16[128,128]{1,0:T(8,128)(2,1)}) custom-call(bf16[128,128]{1,0:T(8,128)(2,1)} %yf_ref.1, bf16[128,128]{1,0:T(8,128)(2,1)} %ys_ref.1, bf16[128,128]{1,0:T(8,128)(2,1)} %gf_ref.1, bf16[128,128]{1,0:T(8,128)(2,1)} %gs_ref.1, ...), custom_call_target="tpu_custom_call" | custom-call | tf_op jit(solution)/shard_map/pallas_call | solution.py:672
  110.6 1.5 %shard_map.193 = (bf16[128,128]{1,0:T(8,128)(2,1)}, bf16[128,128]{1,0:T(8,128)(2,1)}, bf16[128,128]{1,0:T(8,128)(2,1)}, bf16[128,128]{1,0:T(8,128)(2,1)}) custom-call(bf16[128,128]{1,0:T(8,128)(2,1)} %get-tuple-element.8.refs_0_, bf16[128,128]{1,0:T(8,128)(2,1)} %get-tuple-element.9.refs_1_, bf16[128,128]{1,0:T(8,128)(2,1)} %get-tuple-element.10.refs_2_, ...), custom_call_target="tpu_custom_call" | custom-call | tf_op jit(solution)/shard_map/pallas_call | solution.py:755

commit v4 on v3

--- a/solution.py
+++ b/solution.py
@@ -470,31 +470,36 @@
         sums = dot_nn(comb[...], back[...].reshape(n_exp * cap, 512))
         return sums[0:tokens] + sums[tokens : 2 * tokens]
 
-    def to_all(name, ref, ssem, rsem):
-        @pl.when(active)
-        def _():
-            @pl.loop(1, N_CTX)
-            def _(d):
-                remote(ref.at[p], ref.at[p], ssem, rsem.at[p], me, (c + d) % N_CTX).start()
-
-        def sent():
-            pl.when(active)(lambda: wait_bytes(ref.at[pl.ds(0, 7)], ssem))
-
-        def here():
-            pl.when(inactive)(lambda: wait_bytes(ref.at[0], rsem.at[p]))
-            wait_bytes(ref.at[0], rsem.at[1 - p])
-
-        owed[name + " sent"] = sent
-        owed[name] = here
-
     settle("ys", "ret0")
 
     @pl.when(active)
     def _():
         sec[p] = (wide(ys_grp, 4).astype(F32) - combined(out_back)).astype(BF16)
 
-    to_all("sec", sec, sec_s, sec_r)
-    settle("sec")
+    direct = k == qk
+
+    @pl.when(active)
+    def _():
+        @pl.loop(1, 4)
+        def _(d):
+            remote(sec.at[p], sec.at[p], sec_s.at[0], sec_r.at[p], me, (c + 2 * d) % N_CTX).start()
+
+    @pl.when(direct)
+    def _():
+        for h in range(2):
+            pl.when(inactive | (p != h))(functools.partial(wait_bytes, sec.at[h], sec_r.at[h]))
+            remote(sec.at[h], sec.at[h], sec_s.at[1], sec_r.at[h], me, mate).start()
+
+    @pl.when(jnp.logical_not(direct))
+    def _():
+        for h in range(2):
+            wait_bytes(sec.at[h], sec_r.at[h])
+
+    def second_sent():
+        pl.when(active)(lambda: wait_bytes(sec.at[pl.ds(0, 3)], sec_s.at[0]))
+        pl.when(direct)(lambda: wait_bytes(sec.at[pl.ds(0, 2)], sec_s.at[1]))
+
+    owed["sec sent"] = second_sent
     own_lanes = pl.ds(pl.multiple_of(j * 128, 128), 128)
     second_out[...] = sec[p, :, own_lanes]
 
@@ -725,7 +730,7 @@
             dma((4,)),
             dma((2,)),
             dma((2,)),
-            one,
+            dma((2,)),
             dma((2,)),
             one,
             one,

time: 112 us -> 111 us (level)
    pallas_call x1, Pallas kernels: 110 us -> 109 us  [local(): pl.pallas_call(functools.partial(kernel, n_x, n_z, cap), out_shape=(out,)...]
where the time goes in v4:
time: 111 us
  Pallas kernels  110 us (99%)
    pallas_call x1, Pallas kernels, local(): pl.pallas_call(functools.partial(kernel, n_x, n_z, cap), out_shape=(out,)...  109 us

profile of v4, /device:TPU:1, one launch (start us, length us, event | category | flops | bytes accessed | tf_op | source)
XLA Modules:
  0.0 110.9 jit_solution(4977697392964680583)
XLA Ops:
  0.6 108.8 %shard_map.192 = (bf16[128,128]{1,0:T(8,128)(2,1)}, bf16[128,128]{1,0:T(8,128)(2,1)}, bf16[128,128]{1,0:T(8,128)(2,1)}, bf16[128,128]{1,0:T(8,128)(2,1)}) custom-call(bf16[128,128]{1,0:T(8,128)(2,1)} %yf_ref.1, bf16[128,128]{1,0:T(8,128)(2,1)} %ys_ref.1, bf16[128,128]{1,0:T(8,128)(2,1)} %gf_ref.1, bf16[128,128]{1,0:T(8,128)(2,1)} %gs_ref.1, ...), custom_call_target="tpu_custom_call" | custom-call | tf_op jit(solution)/shard_map/pallas_call | solution.py:677
  109.5 1.5 %shard_map.193 = (bf16[128,128]{1,0:T(8,128)(2,1)}, bf16[128,128]{1,0:T(8,128)(2,1)}, bf16[128,128]{1,0:T(8,128)(2,1)}, bf16[128,128]{1,0:T(8,128)(2,1)}) custom-call(bf16[128,128]{1,0:T(8,128)(2,1)} %get-tuple-element.8.refs_0_, bf16[128,128]{1,0:T(8,128)(2,1)} %get-tuple-element.9.refs_1_, bf16[128,128]{1,0:T(8,128)(2,1)} %get-tuple-element.10.refs_2_, ...), custom_call_target="tpu_custom_call" | custom-call | tf_op jit(solution)/shard_map/pallas_call | solution.py:760
